TPU v7x, 128 devices: a whole 4x4x4 slice. The times are simulated.
128 devices in a mesh: dp: 16 (over x, y), seq: 8 (over z, core).
Axes of the slice: x: 4, y: 4, z: 4, core: 2. Of those that a mesh axis runs over, the one named last changes fastest.
Arguments:
- tokens: bfloat16 [16, 512, 2048], P('dp', 'seq'), may hold values from -6 to 6
- memory: bfloat16 [16, 2048, 2048], P('dp', 'seq'), may hold values from -6 to 6
- mem_session: int32 [16, 2048], P('dp', 'seq'), may hold values from 0 to 3, never falling along the last dimension, each value on 1 to 1024 neighbouring positions
- dec_session: int32 [16, 512], P('dp', 'seq'), may hold values from 0 to 3, never falling along the last dimension, each value on 1 to 256 neighbouring positions
- event_bias: float32 [16, 2, 2048], P('dp', None, 'seq'), may hold values from -6 to 263
- expert_ids: int32 [16, 512, 2], P('dp', 'seq'), may hold values from 0 to 23, all different within a row; in each aligned block of 64 rows (0 to 63, 64 to 127, ..., all dimensions but the last counted through in order) at most 6 rows name the same one
- route_weights: float32 [16, 512, 2], P('dp', 'seq'), may hold values from 0.2 to 1
- norm_gain: float32 [2048], replicated, may hold values from 0.25 to 1.75
- w_query: bfloat16 [2048, 1024], P('seq'), may hold values from -0.125 to 0.125
- w_keyval: bfloat16 [2048, 512], P('seq'), may hold values from -0.125 to 0.125
- w_output: bfloat16 [1024, 2048], P('seq'), may hold values from -0.1875 to 0.1875
- w_gate: bfloat16 [24, 2048, 4096], P('seq', None, 'dp'), may hold values from -0.125 to 0.125
- w_up: bfloat16 [24, 2048, 4096], P('seq', None, 'dp'), may hold values from -0.125 to 0.125
- w_down: bfloat16 [24, 4096, 2048], P('seq', 'dp'), may hold values from -0.09375 to 0.09375
- cotangent: bfloat16 [16, 512, 2048], P('dp', 'seq'), may hold values from -6 to 6
Outputs:
- block_out: bfloat16 [16, 512, 2048], P('dp', 'seq')
- grad_resid: bfloat16 [16, 512, 2048], P('dp', 'seq')
- grad_gate: bfloat16 [24, 2048, 4096], P('seq', None, 'dp')
- grad_up: bfloat16 [24, 2048, 4096], P('seq', None, 'dp')
- grad_down: bfloat16 [24, 4096, 2048], P('seq', 'dp')
Inputs may be any that keep to these rules, and one draw needn't show every extreme that they name: `expert_ids`: each token names 2 different experts. Within the tokens of one device (aligned blocks of 64 tokens) no expert is named more than 6 times, a bound that some block reaches. `mem_session`: never falling along the memory rows of one dp index; each of the 4 sessions has 1 to 1024 rows, one exactly 1024. `dec_session`: never falling along the decoder tokens of one dp index; each of the 4 sessions has 1 to 256 tokens, one exactly 256.
All inputs are finite; a program needn't handle non-finite values.
Results may differ from a plain program's by a relative error of at most 0.015.
Values may be sent and summed in bfloat16 or wider, within the bound.
A program may use at most 192 MiB of HBM per device.

v0:
```python
import jax
import jax.numpy as jnp
from jax import lax
from jax.sharding import PartitionSpec as P

D = 2048
EXPERTS = 24
TOPK = 2
QH = 8
KVH = 2
HD = 128
CAP = 6


def attend(queries, key_rows, value_rows, query_session, memory_session, bias_rows):
    token_count = queries.shape[0]
    query_heads = queries.reshape(token_count, KVH, QH // KVH, HD)
    key_heads = key_rows.reshape(-1, KVH, HD)
    value_heads = value_rows.reshape(-1, KVH, HD)
    scores = jnp.einsum(
        "tkgh,mkh->tkgm", query_heads, key_heads, preferred_element_type=jnp.float32
    ) * HD ** (-0.5)
    scores = scores + bias_rows[None, :, None, :]
    same_session = (query_session[:, None] == memory_session[None, :])[:, None, None, :]
    scores = jnp.where(same_session, scores, -1e30)
    row_max = jnp.max(scores, axis=-1, keepdims=True)
    raised = jnp.exp(scores - row_max)
    probability = (raised / jnp.sum(raised, axis=-1, keepdims=True)).astype(jnp.bfloat16)
    attn_mixed = jnp.einsum(
        "tkgm,mkh->tkgh", probability, value_heads, preferred_element_type=jnp.float32
    )
    return attn_mixed.astype(jnp.bfloat16).reshape(token_count, QH * HD)


def per_device(
    tokens,
    memory,
    mem_session,
    dec_session,
    event_bias,
    expert_ids,
    route_weights,
    norm_gain,
    w_query,
    w_keyval,
    w_output,
    w_gate,
    w_up,
    w_down,
    cotangent,
):
    tokens_local = tokens[0]
    kv_width = KVH * HD
    session_all, bias_all = (
        lax.all_gather(mem_session[0], "seq", axis=0, tiled=True),
        lax.all_gather(event_bias[0], "seq", axis=1, tiled=True),
    )
    memory_all, query_weight, keyval_weight, output_weight = (
        lax.all_gather(memory[0], "seq", axis=0, tiled=True),
        lax.all_gather(w_query, "seq", axis=0, tiled=True),
        lax.all_gather(w_keyval, "seq", axis=0, tiled=True),
        lax.all_gather(w_output, "seq", axis=0, tiled=True),
    )
    keyval = jnp.dot(memory_all, keyval_weight, preferred_element_type=jnp.float32).astype(
        jnp.bfloat16
    )
    queries = jnp.dot(tokens_local, query_weight, preferred_element_type=jnp.float32).astype(
        jnp.bfloat16
    )
    attn_mixed = attend(
        queries, keyval[:, :kv_width], keyval[:, kv_width:], dec_session[0], session_all, bias_all
    )
    residual_sum = tokens_local.astype(jnp.float32) + jnp.dot(
        attn_mixed, output_weight, preferred_element_type=jnp.float32
    )
    residual_f = lax.optimization_barrier(residual_sum.astype(jnp.bfloat16)).astype(jnp.float32)
    inv_rms = lax.rsqrt(jnp.mean(residual_f * residual_f, axis=-1, keepdims=True) + 1e-05)
    normed = residual_f * inv_rms
    moe_in = (normed * norm_gain).astype(jnp.bfloat16)
    token_count = tokens_local.shape[0]
    slots_all = EXPERTS * CAP
    expert_flat = expert_ids[0].reshape(-1)
    chosen_mask = expert_flat[:, None] == jnp.arange(EXPERTS, dtype=jnp.int32)[None, :]
    earlier = jnp.cumsum(chosen_mask.astype(jnp.int32), axis=0) - 1
    slot_index = jnp.sum(jnp.where(chosen_mask, earlier, 0), axis=1)
    target = expert_flat * CAP + slot_index
    placer = (jnp.arange(slots_all, dtype=jnp.int32)[:, None] == target[None, :]).astype(
        jnp.bfloat16
    )
    token_placer = jnp.sum(placer.reshape(slots_all, token_count, TOPK), axis=2)
    weights_local = route_weights[0]
    grad_out = (
        (weights_local[:, :, None] * cotangent[0].astype(jnp.float32)[:, None, :])
        .astype(jnp.bfloat16)
        .reshape(token_count * TOPK, D)
    )
    send_in = (
        jnp.dot(token_placer, moe_in, preferred_element_type=jnp.float32)
        .astype(jnp.bfloat16)
        .reshape(EXPERTS, CAP, D)
    )
    send_grad = (
        jnp.dot(placer, grad_out, preferred_element_type=jnp.float32)
        .astype(jnp.bfloat16)
        .reshape(EXPERTS, CAP, D)
    )
    arrived_in, arrived_grad = (
        lax.all_to_all(send_in, "seq", split_axis=0, concat_axis=1, tiled=True),
        lax.all_to_all(send_grad, "seq", split_axis=0, concat_axis=1, tiled=True),
    )
    gathered_in, gathered_grad = (
        lax.all_gather(arrived_in, "dp", axis=1, tiled=True),
        lax.all_gather(arrived_grad, "dp", axis=1, tiled=True),
    )
    gate_pre = jnp.einsum("erd,edf->erf", gathered_in, w_gate, preferred_element_type=jnp.float32)
    up_value = jnp.einsum("erd,edf->erf", gathered_in, w_up, preferred_element_type=jnp.float32)
    sigmoid_gate = jax.nn.sigmoid(gate_pre)
    activated = gate_pre * sigmoid_gate
    hidden = (activated * up_value).astype(jnp.bfloat16)
    partial_out = jnp.einsum("erf,efd->erd", hidden, w_down, preferred_element_type=jnp.float32)
    grad_hidden = jnp.einsum(
        "erd,efd->erf", gathered_grad, w_down, preferred_element_type=jnp.float32
    )
    grad_gate_pre = (
        grad_hidden * up_value * sigmoid_gate * (1.0 + gate_pre * (1.0 - sigmoid_gate))
    ).astype(jnp.bfloat16)
    grad_up_value = (grad_hidden * activated).astype(jnp.bfloat16)
    grad_down = jnp.einsum(
        "erf,erd->efd", hidden, gathered_grad, preferred_element_type=jnp.float32
    ).astype(jnp.bfloat16)
    grad_gate = jnp.einsum(
        "erd,erf->edf", gathered_in, grad_gate_pre, preferred_element_type=jnp.float32
    ).astype(jnp.bfloat16)
    grad_up = jnp.einsum(
        "erd,erf->edf", gathered_in, grad_up_value, preferred_element_type=jnp.float32
    ).astype(jnp.bfloat16)
    partial_grad = jnp.einsum(
        "erf,edf->erd", grad_gate_pre, w_gate, preferred_element_type=jnp.float32
    )
    partial_grad = partial_grad + jnp.einsum(
        "erf,edf->erd", grad_up_value, w_up, preferred_element_type=jnp.float32
    )
    summed_out, summed_grad = (
        lax.psum_scatter(
            partial_out.astype(jnp.bfloat16), "dp", scatter_dimension=1, tiled=True
        ).astype(jnp.float32),
        lax.psum_scatter(
            partial_grad.astype(jnp.bfloat16), "dp", scatter_dimension=1, tiled=True
        ).astype(jnp.float32),
    )
    back_out, back_grad = (
        lax.all_to_all(
            summed_out.astype(jnp.bfloat16), "seq", split_axis=1, concat_axis=0, tiled=True
        ),
        lax.all_to_all(
            summed_grad.astype(jnp.bfloat16), "seq", split_axis=1, concat_axis=0, tiled=True
        ),
    )
    rows_out = jnp.einsum(
        "sr,sd->rd", placer, back_out.reshape(slots_all, D), preferred_element_type=jnp.float32
    ).reshape(token_count, TOPK, D)
    rows_grad = jnp.einsum(
        "sr,sd->rd", placer, back_grad.reshape(slots_all, D), preferred_element_type=jnp.float32
    ).reshape(token_count, TOPK, D)
    block_out = (residual_f + jnp.sum(rows_out * weights_local[:, :, None], axis=1)).astype(
        jnp.bfloat16
    )
    grad_moe = jnp.sum(rows_grad, axis=1)
    grad_normed = grad_moe * norm_gain
    correction = normed * jnp.mean(grad_normed * normed, axis=-1, keepdims=True)
    grad_resid = (cotangent[0].astype(jnp.float32) + inv_rms * (grad_normed - correction)).astype(
        jnp.bfloat16
    )
    return (block_out[None], grad_resid[None], grad_gate, grad_up, grad_down)


def solution(mesh):
    return jax.shard_map(
        per_device,
        mesh=mesh,
        in_specs=(
            P("dp", "seq", None),
            P("dp", "seq", None),
            P("dp", "seq"),
            P("dp", "seq"),
            P("dp", None, "seq"),
            P("dp", "seq", None),
            P("dp", "seq", None),
            P(),
            P("seq", None),
            P("seq", None),
            P("seq", None),
            P("seq", None, "dp"),
            P("seq", None, "dp"),
            P("seq", "dp", None),
            P("dp", "seq", None),
        ),
        out_specs=(
            P("dp", "seq", None),
            P("dp", "seq", None),
            P("seq", None, "dp"),
            P("seq", None, "dp"),
            P("seq", "dp", None),
        ),
        check_vma=False,
    )
```

profile of v0, /device:TPU:1, one launch (start us, length us, event | category | flops | bytes accessed | tf_op | source)
XLA Modules:
  0.0 566.1 jit_solution(12329711389577295675)
XLA Ops:
  11.6 13.4 %all-gather.1 = s32[1,2048]{1,0:T(1,128)S(1)} all-gather(s32[1,256]{1,0:T(1,128)} %param.17), channel_id=3, replica_groups=mesh['dp'=16,'seq'=8] {'seq'}, dimensions={1}, use_global_device_ids=true | all-gather | bytes 9216 | tf_op jit(solution)/shard_map/all_gather | solution.py:55
  25.0 11.3 %all-gather.2 = f32[1,2,2048]{2,1,0:T(2,128)S(1)} all-gather(f32[1,2,256]{2,1,0:T(2,128)} %param.19), channel_id=4, replica_groups=mesh['dp'=16,'seq'=8] {'seq'}, dimensions={2}, use_global_device_ids=true | all-gather | bytes 18432 | tf_op jit(solution)/shard_map/all_gather | solution.py:56
  39.2 6.7 %all-gather.12.cloned.1.call-done = bf16[2048,1024]{1,0:T(8,128)(2,1)} async-done(((bf16[256,1024]{1,0:T(8,128)(2,1)}), bf16[2048,1024]{1,0:T(8,128)(2,1)}) %all-gather.12.cloned.1.call-update) | async-done | bytes 4194320 | tf_op jit(solution)/shard_map/all_gather | solution.py:60
  49.0 23.7 %all-gather.10.cloned.1.call-done = bf16[2048,512]{1,0:T(8,128)(2,1)} async-done(((bf16[256,512]{1,0:T(8,128)(2,1)}), bf16[2048,512]{1,0:T(8,128)(2,1)}) %all-gather.10.cloned.1.call-update) | async-done | bytes 2097168 | tf_op jit(solution)/shard_map/all_gather | solution.py:61
  72.7 52.1 %all-gather.20.cloned.1.call-done = bf16[1,2048,2048]{2,1,0:T(8,128)(2,1)} async-done(((bf16[1,256,2048]{2,1,0:T(8,128)(2,1)}), bf16[1,2048,2048]{2,1,0:T(8,128)(2,1)}) %all-gather.20.cloned.1.call-update) | async-done | bytes 8388624 | tf_op jit(solution)/shard_map/all_gather | solution.py:59
  124.7 8.5 %fusion.4 = bf16[2048,512]{0,1:T(8,128)(2,1)S(1)} fusion(bf16[2048,512]{1,0:T(8,128)(2,1)} %all-gather.10.cloned.1.call-done, bf16[1,2048,2048]{2,1,0:T(8,128)(2,1)} %all-gather.20.cloned.1.call-done), kind=kOutput, calls=%fused_computation.12 | convolution fusion | flops 4296015872 | bytes 12582912 | tf_op jit(solution)/shard_map/dot_general | solution.py:64
  134.8 4.8 fusion.52
  143.1 15.6 %all-gather.14.cloned.1.call-done = bf16[1024,2048]{1,0:T(8,128)(2,1)} async-done(((bf16[128,2048]{1,0:T(8,128)(2,1)}), bf16[1024,2048]{1,0:T(8,128)(2,1)}) %all-gather.14.cloned.1.call-update) | async-done | bytes 4194320 | tf_op jit(solution)/shard_map/all_gather | solution.py:62
  166.0 15.9 %all_to_all.66 = bf16[24,6,2048]{2,1,0:T(8,128)(2,1)S(1)} all-to-all(bf16[24,6,2048]{2,1,0:T(8,128)(2,1)} %reshape.156), channel_id=1, replica_groups=mesh['dp'=16,'seq'=8] {'seq'}, dimensions={0} | all-to-all | bytes 1179648 | tf_op jit(solution)/shard_map/all_to_all | solution.py:108
  195.4 16.7 %all_to_all.67 = bf16[24,6,2048]{2,1,0:T(8,128)(2,1)S(1)} all-to-all(bf16[24,6,2048]{2,1,0:T(8,128)(2,1)} %reshape.158), channel_id=1, replica_groups=mesh['dp'=16,'seq'=8] {'seq'}, dimensions={0} | all-to-all | bytes 1179648 | tf_op jit(solution)/shard_map/all_to_all | solution.py:109
  215.2 45.1 %all-gather.16.cloned.1.call-done = bf16[3,768,2048]{2,1,0:T(8,128)(2,1)} async-done(((bf16[3,48,2048]{2,1,0:T(8,128)(2,1)}), bf16[3,768,2048]{2,1,0:T(8,128)(2,1)}) %all-gather.16.cloned.1.call-update) | async-done | bytes 9437200 | tf_op jit(solution)/shard_map/all_gather | solution.py:112
  260.3 8.7 %fusion.56 = f32[3,768,256]{2,1,0:T(8,128)} fusion(bf16[3,768,2048]{2,1,0:T(8,128)(2,1)} %all-gather.16.cloned.1.call-done, bf16[3,2048,256]{2,1,0:T(8,128)(2,1)} %param.27), kind=kOutput, calls=%fused_computation.84 | convolution fusion | flops 2415919104 | bytes 14942208 | tf_op jit(solution)/shard_map/erd,edf->erf/dot_general | solution.py:116
  273.1 64.6 %all-gather.18.cloned.1.call-done = bf16[3,768,2048]{2,1,0:T(8,128)(2,1)} async-done(((bf16[3,48,2048]{2,1,0:T(8,128)(2,1)}), bf16[3,768,2048]{2,1,0:T(8,128)(2,1)}) %all-gather.18.cloned.1.call-update) | async-done | bytes 9437200 | tf_op jit(solution)/shard_map/all_gather | solution.py:113
  337.6 10.0 %multiply_convert_fusion = (bf16[3,768,256]{2,1,0:T(8,128)(2,1)}, bf16[3,768,256]{2,1,0:T(8,128)(2,1)}, bf16[3,768,256]{2,1,0:T(8,128)(2,1)S(1)}) fusion(f32[3,768,256]{2,1,0:T(8,128)} %fusion.55, f32[3,768,256]{2,1,0:T(8,128)} %fusion.56, bf16[3,768,2048]{2,1,0:T(8,128)(2,1)} %all-gather.18.cloned.1.call-done, bf16[3,256,2048]{2,1,0:T(8,128)(2,1)S(1)} %copy-done), kind=kOutput, calls=%fused_computation.16 | convolution fusion | flops 2424766464 | bytes 20840448 | tf_op jit(solution)/shard_map/erd,efd->erf/dot_general | solution.py:121
  348.7 5.0 convolution_convert_fusion
  354.0 11.7 %fusion.57 = f32[3,768,2048]{2,1,0:T(8,128)} fusion(bf16[3,768,256]{2,1,0:T(8,128)(2,1)} %get-tuple-element.6, bf16[3,2048,256]{2,1,0:T(8,128)(2,1)} %param.26), kind=kOutput, calls=%fused_computation.85 | convolution fusion | flops 2415919104 | bytes 23199744 | tf_op jit(solution)/shard_map/erf,edf->erd/dot_general | solution.py:137
  365.8 11.5 %add_convert_fusion = bf16[3,768,2048]{2,1,0:T(8,128)(2,1)} fusion(f32[3,768,2048]{2,1,0:T(8,128)} %fusion.57, bf16[3,768,256]{2,1,0:T(8,128)(2,1)} %get-tuple-element.5, bf16[3,2048,256]{2,1,0:T(8,128)(2,1)S(1)} %copy-done.2), kind=kOutput, calls=%fused_computation.1 | convolution fusion | flops 2425356288 | bytes 32636928 | tf_op jit(solution)/shard_map/erf,edf->erd/dot_general | solution.py:140
  378.7 9.0 %convolution_convert_fusion.2 = bf16[3,2048,256]{2,1,0:T(8,128)(2,1)} fusion(bf16[3,768,2048]{2,1,0:T(8,128)(2,1)} %all-gather.16.cloned.1.call-done, bf16[3,768,256]{2,1,0:T(8,128)(2,1)S(1)} %copy-done.4), kind=kOutput, calls=%fused_computation.10 | convolution fusion | flops 2417491968 | bytes 13762560 | tf_op jit(solution)/shard_map/erd,erf->edf/dot_general | solution.py:134
  387.7 52.2 %reduce-scatter.3.cloned.1.call-done = bf16[3,48,2048]{2,1,0:T(8,128)(2,1)} async-done(((bf16[3,768,2048]{2,1,0:T(8,128)(2,1)}), bf16[3,48,2048]{2,1,0:T(8,128)(2,1)}) %reduce-scatter.3.cloned.1.call-update) | async-done | bytes 589840 | tf_op jit(solution)/shard_map/reduce_scatter | solution.py:144
  442.3 6.5 %all-to-all-start.1 = ((bf16[3,48,2048]{2,0,1:T(4,128)(2,1)}), bf16[3,48,2048]{2,0,1:T(4,128)(2,1)S(1)}, u32[]{:S(2)}, u32[]{:S(2)}) async-start(bf16[3,48,2048]{2,0,1:T(4,128)(2,1)} %copy.73), calls=%async_computation.2 | async-start | bytes 1572864 | tf_op jit(solution)/shard_map/all_to_all | solution.py:152
  448.8 8.8 %convolution_convert_fusion.3 = bf16[3,2048,256]{2,1,0:T(8,128)(2,1)} fusion(bf16[3,768,2048]{2,1,0:T(8,128)(2,1)} %all-gather.16.cloned.1.call-done, bf16[3,768,256]{2,1,0:T(8,128)(2,1)S(1)} %copy-done.5), kind=kOutput, calls=%fused_computation.11 | convolution fusion | flops 2417491968 | bytes 13762560 | tf_op jit(solution)/shard_map/erd,erf->edf/dot_general | solution.py:131
  457.6 72.6 %reduce-scatter.5.cloned.1.call-done = bf16[3,48,2048]{2,1,0:T(8,128)(2,1)} async-done(((bf16[3,768,2048]{2,1,0:T(8,128)(2,1)}), bf16[3,48,2048]{2,1,0:T(8,128)(2,1)}) %reduce-scatter.5.cloned.1.call-update) | async-done | bytes 589840 | tf_op jit(solution)/shard_map/reduce_scatter | solution.py:147
  532.7 6.2 %all-to-all-start.3 = ((bf16[3,48,2048]{2,0,1:T(4,128)(2,1)}), bf16[3,48,2048]{2,0,1:T(4,128)(2,1)S(1)}, u32[]{:S(2)}, u32[]{:S(2)}) async-start(bf16[3,48,2048]{2,0,1:T(4,128)(2,1)} %copy.79), calls=%async_computation.5 | async-start | bytes 1572864 | tf_op jit(solution)/shard_map/all_to_all | solution.py:155
  538.9 8.4 %convolution_convert_fusion.1 = bf16[3,256,2048]{2,1,0:T(8,128)(2,1)} fusion(bf16[3,768,256]{2,1,0:T(8,128)(2,1)} %copy-done.6, bf16[3,768,2048]{2,1,0:T(8,128)(2,1)} %all-gather.18.cloned.1.call-done), kind=kOutput, calls=%fused_computation.9 | convolution fusion | flops 2417491968 | bytes 13762560 | tf_op jit(solution)/shard_map/erf,erd->efd/dot_general | solution.py:128
  (99 shorter events, 62.2 us)
Async XLA Ops:
  7.2 330.5 %copy-start = (bf16[3,256,2048]{2,1,0:T(8,128)(2,1)S(1)}, bf16[3,256,2048]{2,1,0:T(8,128)(2,1)}, u32[]{:S(2)}) copy-start(bf16[3,256,2048]{2,1,0:T(8,128)(2,1)} %param.28) | copy-start | bytes 9437188
  7.2 38.7 %copy-start.7 = (bf16[1,64,2048]{2,1,0:T(8,128)(2,1)S(1)}, bf16[1,64,2048]{2,1,0:T(8,128)(2,1)}, u32[]{:S(2)}) copy-start(bf16[1,64,2048]{2,1,0:T(8,128)(2,1)} %param.15) | copy-start | bytes 786436
  7.2 38.7 %all-gather.12.cloned.1.call-start = ((), (), s32[]{:S(2)}) async-start(), calls=%async_computation.7 | async-start | bytes 4718592 | tf_op jit(solution)/shard_map/all_gather | solution.py:60
  7.9 64.7 %all-gather.10.cloned.1.call-start = ((), (), s32[]{:S(2)}) async-start(), calls=%async_computation.6 | async-start | bytes 2359296 | tf_op jit(solution)/shard_map/all_gather | solution.py:61
  8.7 116.1 %all-gather.20.cloned.1.call-start = ((), (), s32[]{:S(2)}) async-start(), calls=%async_computation.13 | async-start | bytes 9437184 | tf_op jit(solution)/shard_map/all_gather | solution.py:59
  9.4 149.3 %all-gather.14.cloned.1.call-start = ((), (), s32[]{:S(2)}) async-start(), calls=%async_computation.8 | async-start | bytes 4718592 | tf_op jit(solution)/shard_map/all_gather | solution.py:62
  10.0 250.3 %all-gather.16.cloned.1.call-start = ((), (), s32[]{:S(2)}) async-start(), calls=%async_computation.9 | async-start | bytes 10027008 | tf_op jit(solution)/shard_map/all_gather | solution.py:112
  11.4 27.8 %copy-start.14 = (s32[128]{0:T(128)}, s32[128]{0:T(128)S(1)}, u32[]{:S(2)}) copy-start(s32[128]{0:T(128)S(1)} %select_reduce_fusion) | copy-start | bytes 1540
  133.3 1.5 copy-start.9
  142.9 19.1 %copy-start.10 = (f32[2048]{0:T(1024)S(1)}, f32[2048]{0:T(1024)}, u32[]{:S(2)}) copy-start(f32[2048]{0:T(1024)} %param.22) | copy-start | bytes 24580
  163.9 21.3 %copy-start.13 = (f32[1,64,2]{1,2,0:T(2,128)S(1)}, f32[1,64,2]{1,2,0:T(2,128)}, u32[]{:S(2)}) copy-start(f32[1,64,2]{1,2,0:T(2,128)} %param.21) | copy-start | bytes 1540
  182.8 8.0 %copy-start.12 = (s32[128]{0:T(128)S(1)}, s32[128]{0:T(128)}, u32[]{:S(2)}) copy-start(s32[128]{0:T(128)} %copy-done.11) | copy-start | bytes 1540
  182.8 8.0 %copy-start.15 = (s32[128]{0:T(128)S(1)}, s32[128]{0:T(128)}, u32[]{:S(2)}) copy-start(s32[128]{0:T(128)} %copy-done.14) | copy-start | bytes 1540
  184.9 152.7 %all-gather.18.cloned.1.call-start = ((), (), s32[]{:S(2)}) async-start(), calls=%async_computation.11 | async-start | bytes 10027008 | tf_op jit(solution)/shard_map/all_gather | solution.py:113
  215.1 224.7 %reduce-scatter.3.cloned.1.call-start = ((), (), s32[]{:S(2)}) async-start(), calls=%async_computation.10 | async-start | bytes 10027008 | tf_op jit(solution)/shard_map/reduce_scatter | solution.py:144
  260.3 8.7 %copy-start.3 = (bf16[3,2048,256]{2,1,0:T(8,128)(2,1)S(1)}, bf16[3,2048,256]{2,1,0:T(8,128)(2,1)}, u32[]{:S(2)}) copy-start(bf16[3,2048,256]{2,1,0:T(8,128)(2,1)} %param.26) | copy-start | bytes 9437188
  260.3 8.7 %copy-start.16 = (bf16[3,768,2048]{2,1,0:T(8,128)(2,1)S(1)}, bf16[3,768,2048]{2,1,0:T(8,128)(2,1)}, u32[]{:S(2)}) copy-start(bf16[3,768,2048]{2,1,0:T(8,128)(2,1)} %all-gather.16.cloned.1.call-done) | copy-start | bytes 28311556
  353.7 176.5 %reduce-scatter.5.cloned.1.call-start = ((), (), s32[]{:S(2)}) async-start(), calls=%async_computation.12 | async-start | bytes 10027008 | tf_op jit(solution)/shard_map/reduce_scatter | solution.py:147
  354.0 11.7 %copy-start.2 = (bf16[3,2048,256]{2,1,0:T(8,128)(2,1)S(1)}, bf16[3,2048,256]{2,1,0:T(8,128)(2,1)}, u32[]{:S(2)}) copy-start(bf16[3,2048,256]{2,1,0:T(8,128)(2,1)} %param.27) | copy-start | bytes 9437188
  378.7 70.1 %copy-start.5 = (bf16[3,768,256]{2,1,0:T(8,128)(2,1)S(1)}, bf16[3,768,256]{2,1,0:T(8,128)(2,1)}, u32[]{:S(2)}) copy-start(bf16[3,768,256]{2,1,0:T(8,128)(2,1)} %get-tuple-element.6) | copy-start | bytes 3538948
  442.3 90.3 %all-to-all-start.1 = ((bf16[3,48,2048]{2,0,1:T(4,128)(2,1)}), bf16[3,48,2048]{2,0,1:T(4,128)(2,1)S(1)}, u32[]{:S(2)}, u32[]{:S(2)}) async-start(bf16[3,48,2048]{2,0,1:T(4,128)(2,1)} %copy.73), calls=%async_computation.2 | async-start | bytes 1572864 | tf_op jit(solution)/shard_map/all_to_all | solution.py:152
  532.7 18.5 %all-to-all-start.3 = ((bf16[3,48,2048]{2,0,1:T(4,128)(2,1)}), bf16[3,48,2048]{2,0,1:T(4,128)(2,1)S(1)}, u32[]{:S(2)}, u32[]{:S(2)}) async-start(bf16[3,48,2048]{2,0,1:T(4,128)(2,1)} %copy.79), calls=%async_computation.5 | async-start | bytes 1572864 | tf_op jit(solution)/shard_map/all_to_all | solution.py:155
  552.5 6.3 %copy-start.1 = (bf16[3,256,2048]{2,1,0:T(8,128)(2,1)S(1)}, bf16[3,256,2048]{2,1,0:T(8,128)(2,1)}, u32[]{:S(2)}) copy-start(bf16[3,256,2048]{2,1,0:T(8,128)(2,1)} %param.28) | copy-start | bytes 9437188
  554.7 3.1 copy-start.8
  (3 other events, 3.1 us)
Sparse Core Ops, SparseCore 0:
  9.7 36.0 all-gather.11
  47.6 25.0 all-gather.9
  74.4 50.3 all-gather.19
  126.3 32.3 all-gather.13
  185.0 75.2 all-gather.15
  262.3 75.2 all-gather.17
  353.9 85.9 reduce-scatter.2
  443.7 86.4 reduce-scatter.4
where the time goes:
time: 575 us; the launch traced here: 566 us
  waiting for transfers between devices  338 us (59%)
  matrix products  107 us (19%)
  blocking collectives  57.3 us (10%)
  local copies, waits for them, and re-layouts  30.1 us (5%)
  between operations  14.8 us (3%)
  starting transfers between devices  13.4 us (2%)
  other arithmetic  5.77 us (1%)
    reduce_scatter x1, waiting for transfers between devices, per_device(): lax.psum_scatter(partial_grad.astype(jnp.bfloat16), 'dp', scatter_dimensi...  72.6 us
    all_gather x1, waiting for transfers between devices, per_device(): lax.all_gather(arrived_grad, 'dp', axis=1, tiled=True)  64.6 us
    reduce_scatter x1, waiting for transfers between devices, per_device(): lax.psum_scatter(partial_out.astype(jnp.bfloat16), 'dp', scatter_dimensio...  52.2 us
    all_gather x1, waiting for transfers between devices, per_device(): lax.all_gather(memory[0], 'seq', axis=0, tiled=True)  52.1 us
    all_gather x1, waiting for transfers between devices, per_device(): lax.all_gather(arrived_in, 'dp', axis=1, tiled=True)  45.1 us
    all_gather x1, waiting for transfers between devices, per_device(): lax.all_gather(w_keyval, 'seq', axis=0, tiled=True)  23.7 us
    all_to_all x1, blocking collectives, per_device(): lax.all_to_all(send_grad, 'seq', split_axis=0, concat_axis=1, tiled=True)  16.7 us
    all_to_all x1, blocking collectives, per_device(): lax.all_to_all(send_in, 'seq', split_axis=0, concat_axis=1, tiled=True)  15.9 us
  transfers between devices with their start and end apart: 10, of which 9 were waited for; matrix products, arithmetic and copies ran while one was open for 19% of the time, Pallas kernels for 0%

commit v1 on v0

v1 whole, which is shorter than its diff:
```python
import functools

import jax
import jax.numpy as jnp
import numpy as np
from jax import lax
from jax.experimental import pallas as pl
from jax.experimental.pallas import tpu as pltpu
from jax.sharding import PartitionSpec as P

D = 2048
EXPERTS = 24
TOPK = 2
QH = 8
KVH = 2
HD = 128
CAP = 6
SIDE = 4
N_DP = 16
N_SEQ = 8
OWN = 3
HID = 256
TOK = 64
SRC = N_SEQ * CAP
BLK = 2 * SRC
PACK = 16
MEM = 256
WIDE = D + 256
KV = 2 * KVH * HD
HALF = D // 2
QUARTER = D // 4
MESH = pl.DeviceIdType.MESH
F32 = jnp.float32
BF16 = jnp.bfloat16
NT = (((1,), (1,)), ((), ()))
TN = (((0,), (0,)), ((), ()))


def return_matrix():
    table = np.zeros((BLK, N_SEQ * PACK), np.float32)
    for kind in range(2):
        for source in range(N_SEQ):
            for slot in range(CAP):
                table[kind * SRC + source * CAP + slot, source * PACK + kind * CAP + slot] = 1.0
    return table


def compact_matrix():
    table = np.zeros((OWN * SRC, OWN * SRC), np.float32)
    for expert in range(OWN):
        for source in range(N_SEQ):
            for slot in range(CAP):
                row = expert * CAP + slot
                column = source * 16 + row if row < 16 else N_SEQ * 16 + source * 2 + row - 16
                table[expert * SRC + source * CAP + slot, column] = 1.0
    return table


def corner_matrix():
    table = np.zeros((N_SEQ * 16, N_SEQ * 16), np.float32)
    for piece in range(8):
        for peer in range(N_SEQ):
            for last in range(2):
                table[peer * 16 + piece * 2 + last, piece * 16 + peer * 2 + last] = 1.0
    return table


def add_rows(out, terms):
    @pl.loop(0, BLK // 16)
    def _(i):
        rows = pl.ds(pl.multiple_of(i * 16, 16), 16)
        total = terms[0][rows, :].astype(F32)
        for term in terms[1:]:
            total = total + term[rows, :].astype(F32)
        out[rows, :] = total.astype(BF16)


def block_kernel(
    tokens_ref,
    meta_ref,
    session_ref,
    cot_ref,
    gain_ref,
    weight_ref,
    place_in_ref,
    place_grad_ref,
    select_ref,
    compact_ref,
    corner_ref,
    corner_back_ref,
    expand_ref,
    memory_hbm,
    query_hbm,
    keyval_hbm,
    output_hbm,
    gate_hbm,
    up_hbm,
    down_hbm,
    block_out_ref,
    grad_resid_ref,
    grad_gate_hbm,
    grad_up_hbm,
    grad_down_hbm,
    rows,
    gate_up,
    down,
    hidden,
    grads,
    stage_gate_up,
    memory,
    meta,
    z_send,
    z_recv,
    back_send,
    back_recv,
    first_far,
    first_near,
    second_far,
    second_near,
    residual_keep,
    own_sem,
    load_sem,
    store_sem,
    m_ssem,
    m_rsem,
    w_ssem,
    w_rsem,
    z_ssem,
    z_rsem,
    b_ssem,
    b_rsem,
    g_ssem,
    g_rsem,
    r_ssem,
    r_rsem,
):
    me = lax.axis_index("dp")
    seq = lax.axis_index("seq")
    mx, my = me // SIDE, me % SIDE
    mz, mc = seq // 2, seq % 2
    stage_down = down.at[OWN]

    def device(half, step1, step2):
        dx, dy = (step1, step2) if half == 0 else (step2, step1)
        return ((mx + dx + SIDE) % SIDE) * SIDE + (my + dy + SIDE) % SIDE

    def columns(half):
        return pl.ds(half * HALF, HALF)

    barrier = pltpu.get_barrier_semaphore()
    for half in range(2):
        for step in (1, -1):
            pl.semaphore_signal(
                barrier, inc=1, device_id=(device(half, step, 0), seq), device_id_type=MESH
            )
    for offset in range(1, N_SEQ):
        pl.semaphore_signal(
            barrier, inc=1, device_id=(me, (seq + offset) % N_SEQ), device_id_type=MESH
        )

    def remote(src, dst, ssem, rsem, target):
        copy = pltpu.make_async_remote_copy(
            src_ref=src,
            dst_ref=dst,
            send_sem=ssem,
            recv_sem=rsem,
            device_id=target,
            device_id_type=MESH,
        )
        copy.start()
        return copy

    own_rows = pl.ds(seq * MEM, MEM)
    own_loads = [
        pltpu.make_async_copy(keyval_hbm, gate_up.at[0, own_rows, :], own_sem.at[0]),
        pltpu.make_async_copy(query_hbm.at[:, pl.ds(0, KV)], gate_up.at[1, own_rows, :], own_sem.at[1]),
        pltpu.make_async_copy(query_hbm.at[:, pl.ds(KV, KV)], gate_up.at[2, own_rows, :], own_sem.at[2]),
        pltpu.make_async_copy(output_hbm, down.at[mz, pl.ds(mc * HD, HD), :], own_sem.at[3]),
        pltpu.make_async_copy(memory_hbm, memory, own_sem.at[4]),
    ]
    for copy in own_loads:
        copy.start()

    z_copies = {}

    def exchange_build(kind, place, sources):
        packed = jnp.dot(place[...], sources, preferred_element_type=F32).astype(BF16)
        z_send[kind, :, :, 0:D] = packed[0 : N_SEQ * 16].reshape(N_SEQ, 16, D)
        last = packed[N_SEQ * 16 :]
        pieces = jnp.concatenate([last[:, i * 256 : (i + 1) * 256] for i in range(8)], axis=0)
        corner = jnp.dot(corner_ref[...], pieces, preferred_element_type=F32).astype(BF16)
        z_send[kind, :, :, D:WIDE] = corner.reshape(N_SEQ, 16, 256)

    def exchange_start(kind):
        for offset in range(1, N_SEQ):
            peer = (seq + offset) % N_SEQ
            z_copies[kind, offset] = remote(
                z_send.at[kind, peer],
                z_recv.at[kind, seq],
                z_ssem.at[kind, offset],
                z_rsem.at[kind, offset],
                (me, peer),
            )
        z_recv[kind, seq] = z_send[kind, seq]

    def exchange_end(kind):
        for offset in range(1, N_SEQ):
            z_copies[kind, offset].wait()
        first = z_recv[kind, :, :, 0:D].reshape(N_SEQ * 16, D)
        corner = z_recv[kind, :, :, D:WIDE].reshape(N_SEQ * 16, 256)
        pieces = jnp.dot(corner_back_ref[...], corner, preferred_element_type=F32).astype(BF16)
        last = jnp.concatenate([pieces[i * 16 : (i + 1) * 16] for i in range(8)], axis=1)
        arrived = jnp.concatenate([first, last], axis=0)
        compact = jnp.dot(compact_ref[...], arrived, preferred_element_type=F32).astype(BF16)
        for e in range(OWN):
            rows[e, me, kind * SRC : (kind + 1) * SRC, :] = compact[e * SRC : (e + 1) * SRC]

    ring = {}

    def keyval_weight_region(zz, cc, start, size):
        return gate_up.at[0, pl.ds((zz * 2 + cc) * MEM + start, size), :]

    def query_weight_region(zz, cc, start, size):
        return gate_up.at[pl.ds(1, 2), pl.ds((zz * 2 + cc) * MEM + start, size), :]

    def output_weight_region(zz, cc, start, size):
        return down.at[zz, pl.ds(cc * HD + start, size), :]

    def keyval_region(zz, cc, start, size):
        return stage_gate_up.at[pl.ds((zz * 2 + cc) * MEM + start, size), :]

    regions = [
        (keyval_weight_region, MEM),
        (query_weight_region, MEM),
        (output_weight_region, HD),
        (keyval_region, MEM),
    ]

    def ring_send(which, index, dz_owner, start, size, step, core):
        ref = regions[which][0]((mz + dz_owner + SIDE) % SIDE, mc, start, size)
        target = (me, ((mz + step + SIDE) % SIDE) * 2 + core)
        ring[which, index] = remote(ref, ref, w_ssem.at[which, index], w_rsem.at[which, index], target)

    def ring_1(which):
        size = regions[which][1]
        ring_send(which, 0, 0, 0, size, 1, mc)
        ring_send(which, 1, 0, 0, size, -1, mc)
        ring_send(which, 4, 0, 0, size, 0, 1 - mc)

    def ring_2(which):
        size = regions[which][1]
        ring[which, 0].wait_recv()
        ring_send(which, 2, -1, 0, size // 2, 1, mc)
        ring_send(which, 5, -1, 0, size, 0, 1 - mc)
        ring[which, 1].wait_recv()
        ring_send(which, 3, 1, size // 2, size // 2, -1, mc)
        ring_send(which, 6, 1, 0, size, 0, 1 - mc)

    def ring_3(which):
        ring[which, 2].wait_recv()
        ring[which, 3].wait_recv()
        ring_send(which, 7, 2, 0, regions[which][1], 0, 1 - mc)

    def ring_4(which):
        for index in range(4, 8):
            ring[which, index].wait_recv()

    def ring_sent(which):
        for index in range(8):
            ring[which, index].wait_send()

    def block(half, r1, r2):
        return device(half, r1, r2)

    gathers = {}

    def gather_send(kind, e, half, index, width, origin, steps):
        target = device(half, *steps)
        part = rows.at[e, origin, pl.ds(kind * SRC, SRC), width]
        copy = remote(part, part, g_ssem.at[kind, e, half, index], g_rsem.at[kind, e, half, index], (target, seq))
        gathers[kind, e, half, index] = copy

    def gather_1(kind, e):
        for half in range(2):
            cols = columns(half)
            gather_send(kind, e, half, 0, cols, me, (1, 0))
            gather_send(kind, e, half, 1, cols, me, (-1, 0))
        for half in range(2):
            cols = columns(half)
            gather_send(kind, e, half, 4, cols, me, (0, 1))
            gather_send(kind, e, half, 8, cols, me, (0, -1))

    def gather_2(kind, e):
        for half in range(2):
            cols = columns(half)
            gathers[kind, e, half, 0].wait_recv()
            gather_send(kind, e, half, 2, pl.ds(half * HALF, QUARTER), block(half, -1, 0), (1, 0))
            gathers[kind, e, half, 1].wait_recv()
            gather_send(kind, e, half, 3, pl.ds(half * HALF + QUARTER, QUARTER), block(half, 1, 0), (-1, 0))
            for r in (1, 3):
                gather_send(kind, e, half, 4 + r, cols, block(half, r, 0), (0, 1))
                gather_send(kind, e, half, 8 + r, cols, block(half, r, 0), (0, -1))

    def gather_3(kind, e):
        for half in range(2):
            cols = columns(half)
            gathers[kind, e, half, 2].wait_recv()
            gathers[kind, e, half, 3].wait_recv()
            gather_send(kind, e, half, 6, cols, block(half, 2, 0), (0, 1))
            gather_send(kind, e, half, 10, cols, block(half, 2, 0), (0, -1))

    def gather_4(kind, e):
        for r in (0, 1, 3, 2):
            for half in range(2):
                cols = columns(half)
                gathers[kind, e, half, 4 + r].wait_recv()
                gathers[kind, e, half, 8 + r].wait_recv()
                if r < 2:
                    gather_send(kind, e, half, 12 + r, cols, block(half, r, -1), (0, 1))
                else:
                    gather_send(kind, e, half, 12 + r, cols, block(half, r, 1), (0, -1))

    def gather_5(kind, e):
        for half in range(2):
            for r in range(4):
                gathers[kind, e, half, 12 + r].wait_recv()
            for index in range(16):
                gathers[kind, e, half, index].wait_send()

    loads = []

    def load_start():
        for e in range(OWN):
            loads.append(
                (
                    pltpu.make_async_copy(gate_hbm.at[e], gate_up.at[e, :, pl.ds(0, HID)], load_sem.at[e, 0]),
                    pltpu.make_async_copy(up_hbm.at[e], gate_up.at[e, :, pl.ds(HID, HID)], load_sem.at[e, 1]),
                    pltpu.make_async_copy(down_hbm.at[e], down.at[e], load_sem.at[e, 2]),
                )
            )
        for group in loads:
            for copy in group:
                copy.start()

    stores = {}

    def compute(e):
        for copy in loads[e]:
            copy.wait()
        if e > 0:
            for copy in stores[e - 1]:
                copy.wait()
        group = 8
        tile = group * SRC

        @pl.loop(0, N_DP // group)
        def _(j):
            blocks = pl.ds(j * group, group)
            out_rows = pl.ds(pl.multiple_of(j * tile, tile), tile)
            inputs = rows[e, blocks, 0:SRC, :].reshape(tile, D)
            both = jnp.dot(inputs, gate_up[e], preferred_element_type=F32)
            outer = rows[e, blocks, SRC:BLK, :].reshape(tile, D)
            grad_hidden = lax.dot_general(outer, down[e], NT, preferred_element_type=F32)
            gate_pre, up_value = both[:, :HID], both[:, HID:]
            sigmoid = jax.nn.sigmoid(gate_pre)
            activated = gate_pre * sigmoid
            hidden[out_rows, :] = (activated * up_value).astype(BF16)
            grads[out_rows, 0:HID] = (
                grad_hidden * up_value * sigmoid * (1.0 + gate_pre * (1.0 - sigmoid))
            ).astype(BF16)
            grads[out_rows, HID : 2 * HID] = (grad_hidden * activated).astype(BF16)

        @pl.loop(0, D // 256)
        def _(j):
            cols = pl.ds(pl.multiple_of(j * 256, 256), 256)
            inputs = rows[e, :, 0:SRC, cols].reshape(N_DP * SRC, 256)
            stage_gate_up[cols, :] = lax.dot_general(
                inputs, grads[...], TN, preferred_element_type=F32
            ).astype(BF16)
            outer = rows[e, :, SRC:BLK, cols].reshape(N_DP * SRC, 256)
            down[OWN, :, cols] = lax.dot_general(
                hidden[...], outer, TN, preferred_element_type=F32
            ).astype(BF16)

        stores[e] = (
            pltpu.make_async_copy(stage_gate_up.at[:, pl.ds(0, HID)], grad_gate_hbm.at[e], store_sem.at[e, 0]),
            pltpu.make_async_copy(stage_gate_up.at[:, pl.ds(HID, HID)], grad_up_hbm.at[e], store_sem.at[e, 1]),
            pltpu.make_async_copy(stage_down, grad_down_hbm.at[e], store_sem.at[e, 2]),
        )
        for copy in stores[e]:
            copy.start()

        @pl.loop(0, D // 256)
        def _(j):
            cols = pl.ds(pl.multiple_of(j * 256, 256), 256)
            out = jnp.dot(hidden[...], down[e, :, cols], preferred_element_type=F32)
            rows[e, :, 0:SRC, cols] = out.astype(BF16).reshape(N_DP, SRC, 256)
            back = lax.dot_general(grads[...], gate_up[e, cols, :], NT, preferred_element_type=F32)
            rows[e, :, SRC:BLK, cols] = back.astype(BF16).reshape(N_DP, SRC, 256)

    reduces = {}

    def reduce_send(e, half, index, src, dst, steps):
        target = device(half, *steps)
        copy = remote(src, dst, r_ssem.at[e, half, index], r_rsem.at[e, half, index], (target, seq))
        reduces[e, half, index] = copy

    def part(e, half, r1, r2):
        return rows.at[e, block(half, r1, r2), :, columns(half)]

    def reduce_1(e):
        for half in range(2):
            for r in range(4):
                step = 1 if r < 2 else -1
                reduce_send(e, half, r, part(e, half, r, 2), first_far.at[e, half, r], (0, step))
        for half in range(2):
            for r in (2, 3):
                reduce_send(e, half, 4 + r, part(e, half, r, 1), first_near.at[e, half, 0, r], (0, 1))
            for r in (0, 1):
                reduce_send(e, half, 8 + r, part(e, half, r, -1), first_near.at[e, half, 1, r], (0, -1))

    def reduce_2(e):
        for r in range(4):
            for half in range(2):
                step = 1 if r < 2 else -1
                reduces[e, half, r].wait_recv()
                mine = part(e, half, r, step)
                add_rows(mine, [mine, first_far.at[e, half, r]])
                way = 0 if r < 2 else 1
                reduce_send(
                    e, half, 4 + 4 * way + r, mine, first_near.at[e, half, way, r], (0, step)
                )

    def reduce_3(e):
        for r in (2, 1, 3, 0):
            for half in range(2):
                reduces[e, half, 4 + r].wait_recv()
                reduces[e, half, 8 + r].wait_recv()
                mine = part(e, half, r, 0)
                add_rows(
                    mine, [mine, first_near.at[e, half, 0, r], first_near.at[e, half, 1, r]]
                )
                if r == 2:
                    for way, step in ((0, 1), (1, -1)):
                        quarter = pl.ds(half * HALF + way * QUARTER, QUARTER)
                        src = rows.at[e, block(half, 2, 0), :, quarter]
                        reduce_send(e, half, 12 + way, src, second_far.at[e, half, way], (step, 0))

    def reduce_4(e):
        for half in range(2):
            for way, step in ((0, 1), (1, -1)):
                reduces[e, half, 12 + way].wait_recv()
                quarter = pl.ds(half * HALF + way * QUARTER, QUARTER)
                mine = rows.at[e, block(half, step, 0), :, quarter]
                add_rows(mine, [mine, second_far.at[e, half, way]])
                reduce_send(
                    e, half, 14 + way, part(e, half, step, 0), second_near.at[e, half, way], (step, 0)
                )

    returned = {}

    def reduce_5(e):
        for half in range(2):
            for way in range(2):
                reduces[e, half, 14 + way].wait_recv()
            mine = part(e, half, 0, 0)
            add_rows(mine, [mine, second_near.at[e, half, 0], second_near.at[e, half, 1]])
        back_send[e] = (
            jnp.dot(expand_ref[...], rows[e, me], preferred_element_type=F32)
            .astype(BF16)
            .reshape(N_SEQ, PACK, D)
        )
        for offset in range(1, N_SEQ):
            peer = (seq + offset) % N_SEQ
            returned[e, offset] = remote(
                back_send.at[e, peer],
                back_recv.at[seq, pl.ds(e * PACK, PACK)],
                b_ssem.at[e, offset],
                b_rsem.at[e, offset],
                (me, peer),
            )
        back_recv[seq, e * PACK : (e + 1) * PACK, :] = back_send[e, seq]

    def attention_part(queries, keys, values, bias, same):
        scores = lax.dot_general(queries, keys, NT, preferred_element_type=F32) * HD ** (-0.5)
        scores = jnp.where(same, scores + bias, -1e30)
        row_max = jnp.max(scores, axis=-1, keepdims=True)
        raised = jnp.exp(scores - row_max)
        probability = (raised / jnp.sum(raised, axis=-1, keepdims=True)).astype(BF16)
        return jnp.dot(probability, values, preferred_element_type=F32).astype(BF16)

    cot = cot_ref[...].astype(F32)
    grad0 = (weight_ref[:, 0:1] * cot).astype(BF16)
    grad1 = (weight_ref[:, 1:2] * cot).astype(BF16)
    exchange_build(1, place_grad_ref, jnp.concatenate([grad0, grad1], axis=0))
    meta[seq] = meta_ref[...]
    own_loads[0].wait()
    pl.semaphore_wait(barrier, 4 + N_SEQ - 1)

    exchange_start(1)
    meta_copies = []
    for offset in range(1, N_SEQ):
        peer = (seq + offset) % N_SEQ
        meta_copies.append(
            remote(meta.at[seq], meta.at[seq], m_ssem.at[offset], m_rsem.at[offset], (me, peer))
        )
    ring_1(0)
    for copy in own_loads[1:]:
        copy.wait()
    ring_2(0)
    ring_1(1)
    exchange_end(1)
    for e in range(OWN):
        gather_1(1, e)
    ring_3(0)
    ring_4(0)
    stage_gate_up[own_rows, :] = jnp.dot(
        memory[...], gate_up[0], preferred_element_type=F32
    ).astype(BF16)
    ring_1(3)
    ring_2(1)
    for e in range(OWN):
        gather_2(1, e)
    ring_2(3)
    ring_1(2)
    ring_3(1)
    for e in range(OWN):
        gather_3(1, e)
    ring_3(3)
    ring_4(1)
    tokens = tokens_ref[...]
    queries = [
        jnp.dot(tokens, gate_up[1 + g], preferred_element_type=F32).astype(BF16) for g in range(KVH)
    ]
    for copy in meta_copies:
        copy.wait()
    ring_4(3)
    session_all = jnp.concatenate([meta[s, 2:3, :] for s in range(N_SEQ)], axis=1)
    same = session_ref[...] == session_all
    mixed = []
    for g in range(KVH):
        keys = stage_gate_up[:, g * HD : (g + 1) * HD]
        values = stage_gate_up[:, (KVH + g) * HD : (KVH + g + 1) * HD]
        bias = jnp.concatenate([meta[s, g : g + 1, :] for s in range(N_SEQ)], axis=1)
        for pair in range(2):
            first = queries[g][:, pair * 2 * HD : (pair * 2 + 1) * HD]
            second = queries[g][:, (pair * 2 + 1) * HD : (pair * 2 + 2) * HD]
            both = attention_part(
                jnp.concatenate([first, second], axis=0), keys, values, bias, same
            )
            mixed.extend([both[0:TOK], both[TOK : 2 * TOK]])
        if g == 0:
            ring_2(2)
    ring_3(2)
    ring_4(2)
    mixed = jnp.concatenate(mixed, axis=1)
    projected = jnp.dot(
        mixed, down[...].reshape((OWN + 1) * HID, D), preferred_element_type=F32
    )
    residual_keep[...] = (tokens.astype(F32) + projected).astype(BF16)
    residual = residual_keep[...].astype(F32)
    inv_rms = lax.rsqrt(jnp.mean(residual * residual, axis=-1, keepdims=True) + 1e-05)
    moe_in = (residual * inv_rms * gain_ref[...]).astype(BF16)
    exchange_build(0, place_in_ref, moe_in)
    exchange_start(0)
    for which in range(4):
        ring_sent(which)
    load_start()
    for e in range(OWN):
        gather_4(1, e)
    exchange_end(0)
    for e in range(OWN):
        gather_1(0, e)
    for e in range(OWN):
        gather_2(0, e)
    for e in range(OWN):
        gather_3(0, e)
    for e in range(OWN):
        gather_5(1, e)
    gather_4(0, 0)
    gather_5(0, 0)
    compute(0)
    gather_4(0, 1)
    reduce_1(0)
    gather_5(0, 1)
    compute(1)
    gather_4(0, 2)
    reduce_2(0)
    reduce_1(1)
    gather_5(0, 2)
    compute(2)
    reduce_1(2)
    reduce_2(1)
    reduce_3(0)
    reduce_2(2)
    reduce_4(0)
    reduce_3(1)
    reduce_5(0)
    reduce_4(1)
    reduce_3(2)
    reduce_4(2)
    reduce_5(1)
    reduce_5(2)
    for copy in returned.values():
        copy.wait()
    for copy in reduces.values():
        copy.wait_send()
    for copy in stores[OWN - 1]:
        copy.wait()

    back = back_recv[...].reshape(N_SEQ * OWN * PACK, D)
    picked = jnp.dot(select_ref[...], back, preferred_element_type=F32)
    residual = residual_keep[...].astype(F32)
    block_out_ref[...] = (
        residual
        + (picked[0:TOK] * weight_ref[:, 0:1] + picked[TOK : 2 * TOK] * weight_ref[:, 1:2])
    ).astype(BF16)
    inv_rms = lax.rsqrt(jnp.mean(residual * residual, axis=-1, keepdims=True) + 1e-05)
    normed = residual * inv_rms
    grad_normed = picked[2 * TOK :] * gain_ref[...]
    correction = normed * jnp.mean(grad_normed * normed, axis=-1, keepdims=True)
    grad_resid_ref[...] = (
        cot_ref[...].astype(F32) + inv_rms * (grad_normed - correction)
    ).astype(BF16)


def decoder_block(tokens, memory, meta, session, cot, gain, weights, places, projections, experts):
    vmem = pl.BlockSpec(memory_space=pltpu.VMEM)
    hbm = pl.BlockSpec(memory_space=pl.ANY)
    corner = corner_matrix()
    dma = pltpu.SemaphoreType.DMA
    return pl.pallas_call(
        block_kernel,
        out_shape=(
            jax.ShapeDtypeStruct((TOK, D), BF16),
            jax.ShapeDtypeStruct((TOK, D), BF16),
        )
        + tuple(jax.ShapeDtypeStruct(w.shape, BF16) for w in experts),
        in_specs=[vmem] * 13 + [hbm] * 7,
        out_specs=(vmem, vmem, hbm, hbm, hbm),
        scratch_shapes=[
            pltpu.VMEM((OWN, N_DP, BLK, D), BF16),
            pltpu.VMEM((OWN, D, 2 * HID), BF16),
            pltpu.VMEM((OWN + 1, HID, D), BF16),
            pltpu.VMEM((N_DP * SRC, HID), BF16),
            pltpu.VMEM((N_DP * SRC, 2 * HID), BF16),
            pltpu.VMEM((D, 2 * HID), BF16),
            pltpu.VMEM((MEM, D), BF16),
            pltpu.VMEM((N_SEQ, 8, MEM), F32),
            pltpu.VMEM((2, N_SEQ, 16, WIDE), BF16),
            pltpu.VMEM((2, N_SEQ, 16, WIDE), BF16),
            pltpu.VMEM((OWN, N_SEQ, PACK, D), BF16),
            pltpu.VMEM((N_SEQ, OWN * PACK, D), BF16),
            pltpu.VMEM((OWN, 2, 4, BLK, HALF), BF16),
            pltpu.VMEM((OWN, 2, 2, 4, BLK, HALF), BF16),
            pltpu.VMEM((OWN, 2, 2, BLK, QUARTER), BF16),
            pltpu.VMEM((OWN, 2, 2, BLK, HALF), BF16),
            pltpu.VMEM((TOK, D), BF16),
            dma((5,)),
            dma((OWN, 3)),
            dma((OWN, 3)),
            dma((N_SEQ,)),
            dma((N_SEQ,)),
            dma((4, 8)),
            dma((4, 8)),
            dma((2, N_SEQ)),
            dma((2, N_SEQ)),
            dma((OWN, N_SEQ)),
            dma((OWN, N_SEQ)),
            dma((2, OWN, 2, 16)),
            dma((2, OWN, 2, 16)),
            dma((OWN, 2, 16)),
            dma((OWN, 2, 16)),
        ],
        compiler_params=pltpu.CompilerParams(
            collective_id=1, has_side_effects=True, vmem_limit_bytes=63 * 2**20
        ),
        name="decoder_block",
    )(
        tokens,
        meta,
        session,
        cot,
        gain.reshape(1, D),
        weights,
        *places,
        jnp.asarray(compact_matrix(), BF16),
        jnp.asarray(corner, BF16),
        jnp.asarray(corner.T, BF16),
        jnp.asarray(return_matrix().T, BF16),
        memory,
        *projections,
        *experts,
    )


def routing(expert_ids):
    flat = expert_ids.reshape(-1)
    chosen = flat[:, None] == jnp.arange(EXPERTS, dtype=jnp.int32)[None, :]
    earlier = jnp.cumsum(chosen.astype(jnp.int32), axis=0) - 1
    slot = jnp.sum(jnp.where(chosen, earlier, 0), axis=1)
    owner, place = flat // OWN, (flat % OWN) * CAP + slot
    row = jnp.where(place < 16, owner * 16 + place, N_SEQ * 16 + owner * 2 + place - 16)
    row = row.reshape(-1, TOPK)
    every = jnp.arange(N_SEQ * 18, dtype=jnp.int32)
    sent = [every[:, None] == row[None, :, k] for k in range(TOPK)]
    place_in = (sent[0] | sent[1]).astype(BF16)
    place_grad = jnp.concatenate(sent, axis=1).astype(BF16)
    back = (flat * PACK + slot).reshape(-1, TOPK)
    every = jnp.arange(EXPERTS * PACK, dtype=jnp.int32)
    hit = [every[None, :] == back[:, k : k + 1] for k in range(TOPK)]
    hit_grad = [every[None, :] == back[:, k : k + 1] + CAP for k in range(TOPK)]
    select = jnp.concatenate([hit[0], hit[1], hit_grad[0] | hit_grad[1]], axis=0).astype(BF16)
    return place_in, place_grad, select


def per_device(
    tokens,
    memory,
    mem_session,
    dec_session,
    event_bias,
    expert_ids,
    route_weights,
    norm_gain,
    w_query,
    w_keyval,
    w_output,
    w_gate,
    w_up,
    w_down,
    cotangent,
):
    meta = jnp.concatenate(
        [event_bias[0], mem_session.astype(F32), jnp.zeros((8 - KVH - 1, MEM), F32)], axis=0
    )
    session = jnp.tile(dec_session[0].astype(F32), 2).reshape(2 * TOK, 1)
    block_out, grad_resid, grad_gate, grad_up, grad_down = decoder_block(
        tokens[0],
        memory[0],
        meta,
        session,
        cotangent[0],
        norm_gain,
        route_weights[0],
        routing(expert_ids[0]),
        (w_query, w_keyval, w_output),
        (w_gate, w_up, w_down),
    )
    return (block_out[None], grad_resid[None], grad_gate, grad_up, grad_down)


def solution(mesh):
    return jax.shard_map(
        per_device,
        mesh=mesh,
        in_specs=(
            P("dp", "seq", None),
            P("dp", "seq", None),
            P("dp", "seq"),
            P("dp", "seq"),
            P("dp", None, "seq"),
            P("dp", "seq", None),
            P("dp", "seq", None),
            P(),
            P("seq", None),
            P("seq", None),
            P("seq", None),
            P("seq", None, "dp"),
            P("seq", None, "dp"),
            P("seq", "dp", None),
            P("dp", "seq", None),
        ),
        out_specs=(
            P("dp", "seq", None),
            P("dp", "seq", None),
            P("seq", None, "dp"),
            P("seq", None, "dp"),
            P("seq", "dp", None),
        ),
        check_vma=False,
    )
```

time: 575 us -> 288 us (0.50); the launches traced: 566 us -> 288 us
  waiting for transfers between devices: 338 us -> 0 us
  Pallas kernels: 0 us -> 265 us
  matrix products: 107 us -> 0 us
  blocking collectives: 57.3 us -> 0 us
  local copies, waits for them, and re-layouts: 30.1 us -> 15.4 us
  between operations: 14.8 us -> 0.71 us
  starting transfers between devices: 13.4 us -> 0 us
    pallas_call x0 -> x1, Pallas kernels: none -> 265 us  [decoder_block(): pl.pallas_call(block_kernel, out_shape=(jax.ShapeDtypeStruct((TOK, D), BF...]
    all_gather x6 -> x0, waiting for transfers between devices: 208 us -> none  [the longest x1 64.6 us: per_device(): lax.all_gather(arrived_grad, 'dp', axis=1, tiled=True)]
    reduce_scatter x2 -> x0, waiting for transfers between devices: 125 us -> none  [the longest x1 72.6 us: per_device(): lax.psum_scatter(partial_grad.astype(jnp.bfloat16), 'dp', scatter_dimensi...]
    dot_general x17 -> x0, matrix products: 102 us -> none  [the longest x1 11.7 us: per_device(): jnp.einsum('erf,edf->erd', grad_gate_pre, w_gate, preferred_element_type=...]
    all_to_all x2 -> x0, blocking collectives: 32.6 us -> none  [the longest x1 16.7 us: per_device(): lax.all_to_all(send_grad, 'seq', split_axis=0, concat_axis=1, tiled=True)]
    all_gather x2 -> x0, blocking collectives: 24.7 us -> none  [the longest x1 13.4 us: per_device(): lax.all_gather(mem_session[0], 'seq', axis=0, tiled=True)]
    all_to_all x2 -> x0, starting transfers between devices: 12.7 us -> none  [the longest x1 6.47 us: per_device(): lax.all_to_all(summed_out.astype(jnp.bfloat16), 'seq', split_axis=1, conc...]
    unnamed x36 -> x10, local copies, waits for them, and re-layouts: 3.2 us -> 12.7 us
  transfers between devices with their start and end apart: 10 -> 0, of which waited for: 9 -> 0; matrix products, arithmetic and copies ran while one was open for 19% -> 0% of each run, Pallas kernels for 0% -> 0%
where the time goes in v1:
time: 288 us
  Pallas kernels  265 us (92%)
  local copies, waits for them, and re-layouts  15.4 us (5%)
  other arithmetic  6.9 us (2%)
    pallas_call x1, Pallas kernels, decoder_block(): pl.pallas_call(block_kernel, out_shape=(jax.ShapeDtypeStruct((TOK, D), BF...  265 us
    unnamed x10, local copies, waits for them, and re-layouts  12.7 us

profile of v1, /device:TPU:1, one launch (start us, length us, event | category | flops | bytes accessed | tf_op | source)
XLA Modules:
  0.0 287.7 jit_solution(1887740826704272302)
XLA Ops:
  0.6 0.7 convert_bitcast_fusion
  1.4 0.7 convert_element_type.19
  2.1 0.7 multiply_bitcast_fusion
  2.7 1.3 maximum_maximum_fusion.meta_ref
  4.1 0.1 copy.31
  4.2 1.4 copy.33.weight_ref
  5.6 0.8 copy.29
  6.3 0.1 eq.108
  6.5 0.8 reshape_tile.4.session_ref
  7.3 0.2 reduce_window_sum.11
  7.5 0.2 select_reduce_fusion
  7.7 0.1 reduce_sum.12
  7.9 0.2 slice_reduce_fusion.1
  8.1 0.7 compare_select_fusion
  9.0 0.7 iota_compare_fusion.5
  9.7 0.7 add_convert_fusion.1.place_grad_ref
  10.4 0.7 add_convert_fusion.select_ref
  11.0 264.7 %decoder_block.1 = (bf16[64,2048]{1,0:T(8,128)(2,1)}, bf16[64,2048]{1,0:T(8,128)(2,1)}, bf16[3,2048,256]{2,1,0:T(8,128)(2,1)}, bf16[3,2048,256]{2,1,0:T(8,128)(2,1)}, bf16[3,256,2048]{2,1,0:T(8,128)(2,1)}) custom-call(bf16[64,2048]{1,0:T(8,128)(2,1)} %bitcast.38, f32[8,256]{1,0:T(8,128)} %maximum_maximum_fusion.meta_ref, f32[128,1]{1,0:T(8,128)} %reshape_tile.4.session_ref, ...), custom_call_target="tpu_custom_call" | custom-call | tf_op jit(solution)/shard_map/decoder_block/pallas_call | solution.py:632
  275.8 1.7 copy.39
  277.5 1.7 copy.40
  279.1 3.9 %copy.41 = bf16[3,2048,256]{2,1,0:T(8,128)(2,1)} copy(bf16[3,2048,256]{2,1,0:T(8,128)(2,1)} %get-tuple-element.33) | data formatting | bytes 6291456
  283.0 1.7 copy.42
  284.7 1.4 copy-done
  286.1 1.7 copy.43
  (12 shorter events, 0.4 us)
Async XLA Ops:
  279.1 3.9 %copy-start.1 = (bf16[3,2048,256]{2,1,0:T(8,128)(2,1)S(1)}, bf16[3,2048,256]{2,1,0:T(8,128)(2,1)}, u32[]{:S(2)}) copy-start(bf16[3,2048,256]{2,1,0:T(8,128)(2,1)} %get-tuple-element.34) | copy-start | bytes 9437188
  283.0 3.0 %copy-start = (bf16[3,256,2048]{2,1,0:T(8,128)(2,1)S(1)}, bf16[3,256,2048]{2,1,0:T(8,128)(2,1)}, u32[]{:S(2)}) copy-start(bf16[3,256,2048]{2,1,0:T(8,128)(2,1)} %get-tuple-element.35) | copy-start | bytes 9437188

commit v2 on v1

--- a/solution.py
+++ b/solution.py
@@ -65,6 +65,49 @@
     return table
 
 
+def squares():
+    down = lax.broadcasted_iota(jnp.int32, (TOK, TOK), 0)
+    across = lax.broadcasted_iota(jnp.int32, (TOK, TOK), 1)
+    return down, across
+
+
+def as_column(row):
+    down, across = squares()
+    return jnp.sum(jnp.where(down == across, row, 0.0), axis=1, keepdims=True)
+
+
+def one_hot(mask):
+    return jnp.where(mask, 1.0, 0.0).astype(BF16)
+
+
+def routed(ids_ref):
+    down, across = squares()
+    row = [ids_ref[k : k + 1, :].astype(F32) for k in range(TOPK)]
+    column = [as_column(r) for r in row]
+
+    def earlier(own, others, before, axis):
+        named = sum(jnp.where(own == other, 1.0, 0.0) for other in others)
+        return jnp.sum(jnp.where(before, named, 0.0), axis=axis, keepdims=True)
+
+    row_slot = [earlier(row[k], column, down < across, 0) for k in range(TOPK)]
+    column_slot = [earlier(column[k], row, across < down, 1) for k in range(TOPK)]
+    return row, row_slot, column, column_slot
+
+
+def send_places(ids_ref):
+    row, row_slot, _, _ = routed(ids_ref)
+    every = lax.broadcasted_iota(jnp.int32, (N_SEQ * 18, TOK), 0).astype(F32)
+    places = []
+    for k in range(TOPK):
+        owner = jnp.floor((row[k] + 0.5) * (1.0 / OWN))
+        place = (row[k] - OWN * owner) * CAP + row_slot[k]
+        target = jnp.where(
+            place < 16, owner * 16 + place, N_SEQ * 16 + owner * 2 + place - 16
+        )
+        places.append(jnp.where(every == target, 1.0, 0.0))
+    return places
+
+
 def add_rows(out, terms):
     @pl.loop(0, BLK // 16)
     def _(i):
@@ -75,16 +118,62 @@
         out[rows, :] = total.astype(BF16)
 
 
+def finish_kernel(
+    ids_ref,
+    weight_ref,
+    back_ref,
+    residual_ref,
+    cot_ref,
+    gain_ref,
+    gate_in,
+    up_in,
+    down_in,
+    block_out_ref,
+    grad_resid_ref,
+    gate_out,
+    up_out,
+    down_out,
+    sem,
+):
+    copies = []
+    for e in range(OWN):
+        for i, (src, dst) in enumerate(((gate_in, gate_out), (up_in, up_out), (down_in, down_out))):
+            copies.append(pltpu.make_async_copy(src.at[e], dst.at[e], sem.at[e, i]))
+    for copy in copies:
+        copy.start()
+    _, _, column, column_slot = routed(ids_ref)
+    every = lax.broadcasted_iota(jnp.int32, (TOK, EXPERTS * PACK), 1).astype(F32)
+    back = back_ref[...].reshape(EXPERTS * PACK, D)
+    answers = [column[k] * PACK + column_slot[k] for k in range(TOPK)]
+    residual = residual_ref[...].astype(F32)
+    combined = None
+    for k in range(TOPK):
+        picked = jnp.dot(one_hot(every == answers[k]), back, preferred_element_type=F32)
+        term = picked * as_column(weight_ref[k : k + 1, :])
+        combined = term if combined is None else combined + term
+    block_out_ref[...] = (residual + combined).astype(BF16)
+    both = (every == answers[0] + CAP) | (every == answers[1] + CAP)
+    grad_moe = jnp.dot(one_hot(both), back, preferred_element_type=F32)
+    inv_rms = lax.rsqrt(jnp.mean(residual * residual, axis=-1, keepdims=True) + 1e-05)
+    normed = residual * inv_rms
+    grad_normed = grad_moe * gain_ref[...]
+    correction = normed * jnp.mean(grad_normed * normed, axis=-1, keepdims=True)
+    grad_resid_ref[...] = (
+        cot_ref[...].astype(F32) + inv_rms * (grad_normed - correction)
+    ).astype(BF16)
+    for copy in copies:
+        copy.wait()
+
+
 def block_kernel(
     tokens_ref,
-    meta_ref,
+    bias_ref,
+    mem_session_ref,
     session_ref,
     cot_ref,
     gain_ref,
+    ids_ref,
     weight_ref,
-    place_in_ref,
-    place_grad_ref,
-    select_ref,
     compact_ref,
     corner_ref,
     corner_back_ref,
@@ -96,8 +185,8 @@
     gate_hbm,
     up_hbm,
     down_hbm,
-    block_out_ref,
-    grad_resid_ref,
+    back_recv,
+    residual_keep,
     grad_gate_hbm,
     grad_up_hbm,
     grad_down_hbm,
@@ -112,12 +201,10 @@
     z_send,
     z_recv,
     back_send,
-    back_recv,
     first_far,
     first_near,
     second_far,
     second_near,
-    residual_keep,
     own_sem,
     load_sem,
     store_sem,
@@ -183,8 +270,7 @@
 
     z_copies = {}
 
-    def exchange_build(kind, place, sources):
-        packed = jnp.dot(place[...], sources, preferred_element_type=F32).astype(BF16)
+    def exchange_build(kind, packed):
         z_send[kind, :, :, 0:D] = packed[0 : N_SEQ * 16].reshape(N_SEQ, 16, D)
         last = packed[N_SEQ * 16 :]
         pieces = jnp.concatenate([last[:, i * 256 : (i + 1) * 256] for i in range(8)], axis=0)
@@ -489,11 +575,18 @@
         probability = (raised / jnp.sum(raised, axis=-1, keepdims=True)).astype(BF16)
         return jnp.dot(probability, values, preferred_element_type=F32).astype(BF16)
 
+    places = send_places(ids_ref)
     cot = cot_ref[...].astype(F32)
-    grad0 = (weight_ref[:, 0:1] * cot).astype(BF16)
-    grad1 = (weight_ref[:, 1:2] * cot).astype(BF16)
-    exchange_build(1, place_grad_ref, jnp.concatenate([grad0, grad1], axis=0))
-    meta[seq] = meta_ref[...]
+    packed = None
+    for k in range(TOPK):
+        grad_out = (as_column(weight_ref[k : k + 1, :]) * cot).astype(BF16)
+        term = jnp.dot(places[k].astype(BF16), grad_out, preferred_element_type=F32)
+        packed = term if packed is None else packed + term
+    exchange_build(1, packed.astype(BF16))
+    meta[seq] = jnp.concatenate(
+        [bias_ref[...], mem_session_ref[...].astype(F32), jnp.zeros((8 - KVH - 1, MEM), F32)],
+        axis=0,
+    )
     own_loads[0].wait()
     pl.semaphore_wait(barrier, 4 + N_SEQ - 1)
 
@@ -536,7 +629,8 @@
         copy.wait()
     ring_4(3)
     session_all = jnp.concatenate([meta[s, 2:3, :] for s in range(N_SEQ)], axis=1)
-    same = session_ref[...] == session_all
+    own_session = as_column(session_ref[...].astype(F32))
+    same = jnp.concatenate([own_session, own_session], axis=0) == session_all
     mixed = []
     for g in range(KVH):
         keys = stage_gate_up[:, g * HD : (g + 1) * HD]
@@ -561,7 +655,8 @@
     residual = residual_keep[...].astype(F32)
     inv_rms = lax.rsqrt(jnp.mean(residual * residual, axis=-1, keepdims=True) + 1e-05)
     moe_in = (residual * inv_rms * gain_ref[...]).astype(BF16)
-    exchange_build(0, place_in_ref, moe_in)
+    either = (places[0] + places[1]).astype(BF16)
+    exchange_build(0, jnp.dot(either, moe_in, preferred_element_type=F32).astype(BF16))
     exchange_start(0)
     for which in range(4):
         ring_sent(which)
@@ -569,19 +664,22 @@
     for e in range(OWN):
         gather_4(1, e)
     exchange_end(0)
-    for e in range(OWN):
-        gather_1(0, e)
-    for e in range(OWN):
-        gather_2(0, e)
-    for e in range(OWN):
-        gather_3(0, e)
+    gather_1(0, 0)
+    gather_1(0, 1)
+    gather_2(0, 0)
+    gather_3(0, 0)
+    gather_1(0, 2)
+    gather_2(0, 1)
+    gather_4(0, 0)
+    gather_3(0, 1)
     for e in range(OWN):
         gather_5(1, e)
-    gather_4(0, 0)
     gather_5(0, 0)
     compute(0)
     gather_4(0, 1)
     reduce_1(0)
+    gather_2(0, 2)
+    gather_3(0, 2)
     gather_5(0, 1)
     compute(1)
     gather_4(0, 2)
@@ -608,23 +706,28 @@
     for copy in stores[OWN - 1]:
         copy.wait()
 
-    back = back_recv[...].reshape(N_SEQ * OWN * PACK, D)
-    picked = jnp.dot(select_ref[...], back, preferred_element_type=F32)
-    residual = residual_keep[...].astype(F32)
-    block_out_ref[...] = (
-        residual
-        + (picked[0:TOK] * weight_ref[:, 0:1] + picked[TOK : 2 * TOK] * weight_ref[:, 1:2])
-    ).astype(BF16)
-    inv_rms = lax.rsqrt(jnp.mean(residual * residual, axis=-1, keepdims=True) + 1e-05)
-    normed = residual * inv_rms
-    grad_normed = picked[2 * TOK :] * gain_ref[...]
-    correction = normed * jnp.mean(grad_normed * normed, axis=-1, keepdims=True)
-    grad_resid_ref[...] = (
-        cot_ref[...].astype(F32) + inv_rms * (grad_normed - correction)
-    ).astype(BF16)
-
-
-def decoder_block(tokens, memory, meta, session, cot, gain, weights, places, projections, experts):
+
+def finish(ids, weights, back, residual, cot, gain, grads):
+    vmem = pl.BlockSpec(memory_space=pltpu.VMEM)
+    hbm = pl.BlockSpec(memory_space=pl.ANY)
+    return pl.pallas_call(
+        finish_kernel,
+        out_shape=(
+            jax.ShapeDtypeStruct((TOK, D), BF16),
+            jax.ShapeDtypeStruct((TOK, D), BF16),
+        )
+        + tuple(jax.ShapeDtypeStruct(g.shape, BF16) for g in grads),
+        in_specs=[vmem] * 6 + [hbm] * 3,
+        out_specs=(vmem, vmem, hbm, hbm, hbm),
+        scratch_shapes=[pltpu.SemaphoreType.DMA((OWN, 3))],
+        compiler_params=pltpu.CompilerParams(vmem_limit_bytes=63 * 2**20),
+        name="finish",
+    )(ids, weights, back, residual, cot, gain, *grads)
+
+
+def decoder_block(
+    tokens, memory, bias, mem_session, session, cot, gain, ids, weights, projections, experts
+):
     vmem = pl.BlockSpec(memory_space=pltpu.VMEM)
     hbm = pl.BlockSpec(memory_space=pl.ANY)
     corner = corner_matrix()
@@ -632,11 +735,11 @@
     return pl.pallas_call(
         block_kernel,
         out_shape=(
-            jax.ShapeDtypeStruct((TOK, D), BF16),
+            jax.ShapeDtypeStruct((N_SEQ, OWN * PACK, D), BF16),
             jax.ShapeDtypeStruct((TOK, D), BF16),
         )
         + tuple(jax.ShapeDtypeStruct(w.shape, BF16) for w in experts),
-        in_specs=[vmem] * 13 + [hbm] * 7,
+        in_specs=[vmem] * 12 + [hbm] * 7,
         out_specs=(vmem, vmem, hbm, hbm, hbm),
         scratch_shapes=[
             pltpu.VMEM((OWN, N_DP, BLK, D), BF16),
@@ -650,12 +753,10 @@
             pltpu.VMEM((2, N_SEQ, 16, WIDE), BF16),
             pltpu.VMEM((2, N_SEQ, 16, WIDE), BF16),
             pltpu.VMEM((OWN, N_SEQ, PACK, D), BF16),
-            pltpu.VMEM((N_SEQ, OWN * PACK, D), BF16),
             pltpu.VMEM((OWN, 2, 4, BLK, HALF), BF16),
             pltpu.VMEM((OWN, 2, 2, 4, BLK, HALF), BF16),
             pltpu.VMEM((OWN, 2, 2, BLK, QUARTER), BF16),
             pltpu.VMEM((OWN, 2, 2, BLK, HALF), BF16),
-            pltpu.VMEM((TOK, D), BF16),
             dma((5,)),
             dma((OWN, 3)),
             dma((OWN, 3)),
@@ -678,12 +779,13 @@
         name="decoder_block",
     )(
         tokens,
-        meta,
+        bias,
+        mem_session,
         session,
         cot,
-        gain.reshape(1, D),
+        gain,
+        ids,
         weights,
-        *places,
         jnp.asarray(compact_matrix(), BF16),
         jnp.asarray(corner, BF16),
         jnp.asarray(corner.T, BF16),
@@ -692,26 +794,6 @@
         *projections,
         *experts,
     )
-
-
-def routing(expert_ids):
-    flat = expert_ids.reshape(-1)
-    chosen = flat[:, None] == jnp.arange(EXPERTS, dtype=jnp.int32)[None, :]
-    earlier = jnp.cumsum(chosen.astype(jnp.int32), axis=0) - 1
-    slot = jnp.sum(jnp.where(chosen, earlier, 0), axis=1)
-    owner, place = flat // OWN, (flat % OWN) * CAP + slot
-    row = jnp.where(place < 16, owner * 16 + place, N_SEQ * 16 + owner * 2 + place - 16)
-    row = row.reshape(-1, TOPK)
-    every = jnp.arange(N_SEQ * 18, dtype=jnp.int32)
-    sent = [every[:, None] == row[None, :, k] for k in range(TOPK)]
-    place_in = (sent[0] | sent[1]).astype(BF16)
-    place_grad = jnp.concatenate(sent, axis=1).astype(BF16)
-    back = (flat * PACK + slot).reshape(-1, TOPK)
-    every = jnp.arange(EXPERTS * PACK, dtype=jnp.int32)
-    hit = [every[None, :] == back[:, k : k + 1] for k in range(TOPK)]
-    hit_grad = [every[None, :] == back[:, k : k + 1] + CAP for k in range(TOPK)]
-    select = jnp.concatenate([hit[0], hit[1], hit_grad[0] | hit_grad[1]], axis=0).astype(BF16)
-    return place_in, place_grad, select
 
 
 def per_device(
@@ -731,21 +813,23 @@
     w_down,
     cotangent,
 ):
-    meta = jnp.concatenate(
-        [event_bias[0], mem_session.astype(F32), jnp.zeros((8 - KVH - 1, MEM), F32)], axis=0
-    )
-    session = jnp.tile(dec_session[0].astype(F32), 2).reshape(2 * TOK, 1)
-    block_out, grad_resid, grad_gate, grad_up, grad_down = decoder_block(
+    ids, weights = expert_ids[0].T, route_weights[0].T
+    gain = norm_gain.reshape(1, D)
+    back, residual, *grads = decoder_block(
         tokens[0],
         memory[0],
-        meta,
-        session,
+        event_bias[0],
+        mem_session,
+        dec_session,
         cotangent[0],
-        norm_gain,
-        route_weights[0],
-        routing(expert_ids[0]),
+        gain,
+        ids,
+        weights,
         (w_query, w_keyval, w_output),
         (w_gate, w_up, w_down),
+    )
+    block_out, grad_resid, grad_gate, grad_up, grad_down = finish(
+        ids, weights, back, residual, cotangent[0], gain, grads
     )
     return (block_out[None], grad_resid[None], grad_gate, grad_up, grad_down)
 

time: 288 us -> 566 us (1.97)
  Pallas kernels: 265 us -> 565 us
  local copies, waits for them, and re-layouts: 15.4 us -> 0 us
  other arithmetic: 6.9 us -> 0 us
    pallas_call x1 -> x2, Pallas kernels: 265 us -> 565 us  [the longest x1 289 us: finish(): pl.pallas_call(finish_kernel, out_shape=(jax.ShapeDtypeStruct((TOK, D), B...]
    unnamed x10 -> x0, local copies, waits for them, and re-layouts: 12.7 us -> none
where the time goes in v2:
time: 566 us
  Pallas kernels  565 us (100%)
    pallas_call x1, Pallas kernels, finish(): pl.pallas_call(finish_kernel, out_shape=(jax.ShapeDtypeStruct((TOK, D), B...  289 us
    pallas_call x1, Pallas kernels, decoder_block(): pl.pallas_call(block_kernel, out_shape=(jax.ShapeDtypeStruct((N_SEQ, OWN...  276 us

profile of v2, /device:TPU:1, one launch (start us, length us, event | category | flops | bytes accessed | tf_op | source)
XLA Modules:
  0.0 565.7 jit_solution(7075610479838696812)
XLA Ops:
  0.6 275.5 %decoder_block.1 = (bf16[8,48,2048]{2,1,0:T(8,128)(2,1)}, bf16[64,2048]{1,0:T(8,128)(2,1)}, bf16[3,2048,256]{2,1,0:T(8,128)(2,1)}, bf16[3,2048,256]{2,1,0:T(8,128)(2,1)}, bf16[3,256,2048]{2,1,0:T(8,128)(2,1)}) custom-call(bf16[64,2048]{1,0:T(8,128)(2,1)} %bitcast.16, f32[2,256]{1,0:T(2,128)} %bitcast.23, s32[1,256]{1,0:T(1,128)} %mem_session_ref.1, ...), custom_call_target="tpu_custom_call" | custom-call | tf_op jit(solution)/shard_map/decoder_block/pallas_call | solution.py:735
  276.2 289.4 %finish.1 = (bf16[64,2048]{1,0:T(8,128)(2,1)}, bf16[64,2048]{1,0:T(8,128)(2,1)}, bf16[3,2048,256]{2,1,0:T(8,128)(2,1)}, bf16[3,2048,256]{2,1,0:T(8,128)(2,1)}, bf16[3,256,2048]{2,1,0:T(8,128)(2,1)}) custom-call(s32[2,64]{1,0:T(2,128)} %bitcast.20, f32[2,64]{1,0:T(2,128)} %bitcast.22, bf16[8,48,2048]{2,1,0:T(8,128)(2,1)} %get-tuple-element.15.back_ref, ...), custom_call_target="tpu_custom_call" | custom-call | tf_op jit(solution)/shard_map/finish/pallas_call | solution.py:713

commit v3 on v2

--- a/solution.py
+++ b/solution.py
@@ -133,13 +133,23 @@
     gate_out,
     up_out,
     down_out,
-    sem,
+    gate_via,
+    up_via,
+    down_via,
+    in_sem,
+    out_sem,
 ):
-    copies = []
+    loads, copies = [], []
     for e in range(OWN):
-        for i, (src, dst) in enumerate(((gate_in, gate_out), (up_in, up_out), (down_in, down_out))):
-            copies.append(pltpu.make_async_copy(src.at[e], dst.at[e], sem.at[e, i]))
-    for copy in copies:
+        for i, (src, via, dst) in enumerate(
+            ((gate_in, gate_via, gate_out), (up_in, up_via, up_out), (down_in, down_via, down_out))
+        ):
+            loads.append(pltpu.make_async_copy(src.at[e], via.at[e], in_sem.at[e, i]))
+            copies.append(pltpu.make_async_copy(via.at[e], dst.at[e], out_sem.at[e, i]))
+    for load in loads:
+        load.start()
+    for load, copy in zip(loads, copies):
+        load.wait()
         copy.start()
     _, _, column, column_slot = routed(ids_ref)
     every = lax.broadcasted_iota(jnp.int32, (TOK, EXPERTS * PACK), 1).astype(F32)
@@ -666,23 +676,23 @@
     exchange_end(0)
     gather_1(0, 0)
     gather_1(0, 1)
+    gather_1(0, 2)
     gather_2(0, 0)
+    gather_2(0, 1)
+    gather_2(0, 2)
     gather_3(0, 0)
-    gather_1(0, 2)
-    gather_2(0, 1)
-    gather_4(0, 0)
     gather_3(0, 1)
+    gather_3(0, 2)
     for e in range(OWN):
         gather_5(1, e)
+    gather_4(0, 0)
+    gather_4(0, 1)
+    gather_4(0, 2)
     gather_5(0, 0)
     compute(0)
-    gather_4(0, 1)
     reduce_1(0)
-    gather_2(0, 2)
-    gather_3(0, 2)
     gather_5(0, 1)
     compute(1)
-    gather_4(0, 2)
     reduce_2(0)
     reduce_1(1)
     gather_5(0, 2)
@@ -719,7 +729,8 @@
         + tuple(jax.ShapeDtypeStruct(g.shape, BF16) for g in grads),
         in_specs=[vmem] * 6 + [hbm] * 3,
         out_specs=(vmem, vmem, hbm, hbm, hbm),
-        scratch_shapes=[pltpu.SemaphoreType.DMA((OWN, 3))],
+        scratch_shapes=[pltpu.VMEM(g.shape, BF16) for g in grads]
+        + [pltpu.SemaphoreType.DMA((OWN, 3)), pltpu.SemaphoreType.DMA((OWN, 3))],
         compiler_params=pltpu.CompilerParams(vmem_limit_bytes=63 * 2**20),
         name="finish",
     )(ids, weights, back, residual, cot, gain, *grads)

time: 566 us -> 268 us (0.47)
  Pallas kernels: 565 us -> 267 us
    pallas_call x1, Pallas kernels: 289 us -> 9.79 us  [finish(): pl.pallas_call(finish_kernel, out_shape=(jax.ShapeDtypeStruct((TOK, D), B...]
    pallas_call x1, Pallas kernels: 276 us -> 257 us  [decoder_block(): pl.pallas_call(block_kernel, out_shape=(jax.ShapeDtypeStruct((N_SEQ, OWN...]
where the time goes in v3:
time: 268 us
  Pallas kernels  267 us (100%)
    pallas_call x1, Pallas kernels, decoder_block(): pl.pallas_call(block_kernel, out_shape=(jax.ShapeDtypeStruct((N_SEQ, OWN...  257 us
    pallas_call x1, Pallas kernels, finish(): pl.pallas_call(finish_kernel, out_shape=(jax.ShapeDtypeStruct((TOK, D), B...  9.79 us

profile of v3, /device:TPU:1, one launch (start us, length us, event | category | flops | bytes accessed | tf_op | source)
XLA Modules:
  0.0 267.9 jit_solution(5291569114821494901)
XLA Ops:
  0.6 257.3 %decoder_block.1 = (bf16[8,48,2048]{2,1,0:T(8,128)(2,1)}, bf16[64,2048]{1,0:T(8,128)(2,1)}, bf16[3,2048,256]{2,1,0:T(8,128)(2,1)}, bf16[3,2048,256]{2,1,0:T(8,128)(2,1)}, bf16[3,256,2048]{2,1,0:T(8,128)(2,1)}) custom-call(bf16[64,2048]{1,0:T(8,128)(2,1)} %bitcast.16, f32[2,256]{1,0:T(2,128)} %bitcast.23, s32[1,256]{1,0:T(1,128)} %mem_session_ref.1, ...), custom_call_target="tpu_custom_call" | custom-call | tf_op jit(solution)/shard_map/decoder_block/pallas_call | solution.py:746
  258.0 9.8 %finish.1 = (bf16[64,2048]{1,0:T(8,128)(2,1)}, bf16[64,2048]{1,0:T(8,128)(2,1)}, bf16[3,2048,256]{2,1,0:T(8,128)(2,1)}, bf16[3,2048,256]{2,1,0:T(8,128)(2,1)}, bf16[3,256,2048]{2,1,0:T(8,128)(2,1)}) custom-call(s32[2,64]{1,0:T(2,128)} %bitcast.20, f32[2,64]{1,0:T(2,128)} %bitcast.22, bf16[8,48,2048]{2,1,0:T(8,128)(2,1)} %get-tuple-element.15.back_ref, ...), custom_call_target="tpu_custom_call" | custom-call | tf_op jit(solution)/shard_map/finish/pallas_call | solution.py:723

commit v4 on v3

--- a/solution.py
+++ b/solution.py
@@ -27,6 +27,7 @@
 MEM = 256
 WIDE = D + 256
 KV = 2 * KVH * HD
+STRIP = HD // 4
 HALF = D // 2
 QUARTER = D // 4
 MESH = pl.DeviceIdType.MESH
@@ -148,9 +149,6 @@
             copies.append(pltpu.make_async_copy(via.at[e], dst.at[e], out_sem.at[e, i]))
     for load in loads:
         load.start()
-    for load, copy in zip(loads, copies):
-        load.wait()
-        copy.start()
     _, _, column, column_slot = routed(ids_ref)
     every = lax.broadcasted_iota(jnp.int32, (TOK, EXPERTS * PACK), 1).astype(F32)
     back = back_ref[...].reshape(EXPERTS * PACK, D)
@@ -171,6 +169,9 @@
     grad_resid_ref[...] = (
         cot_ref[...].astype(F32) + inv_rms * (grad_normed - correction)
     ).astype(BF16)
+    for load, copy in zip(loads, copies):
+        load.wait()
+        copy.start()
     for copy in copies:
         copy.wait()
 
@@ -220,6 +221,8 @@
     store_sem,
     m_ssem,
     m_rsem,
+    s_ssem,
+    s_rsem,
     w_ssem,
     w_rsem,
     z_ssem,
@@ -246,7 +249,7 @@
 
     barrier = pltpu.get_barrier_semaphore()
     for half in range(2):
-        for step in (1, -1):
+        for step in (1, -1, 2):
             pl.semaphore_signal(
                 barrier, inc=1, device_id=(device(half, step, 0), seq), device_id_type=MESH
             )
@@ -319,16 +322,13 @@
     def query_weight_region(zz, cc, start, size):
         return gate_up.at[pl.ds(1, 2), pl.ds((zz * 2 + cc) * MEM + start, size), :]
 
-    def output_weight_region(zz, cc, start, size):
-        return down.at[zz, pl.ds(cc * HD + start, size), :]
-
     def keyval_region(zz, cc, start, size):
         return stage_gate_up.at[pl.ds((zz * 2 + cc) * MEM + start, size), :]
 
     regions = [
         (keyval_weight_region, MEM),
         (query_weight_region, MEM),
-        (output_weight_region, HD),
+        None,
         (keyval_region, MEM),
     ]
 
@@ -364,6 +364,74 @@
     def ring_sent(which):
         for index in range(8):
             ring[which, index].wait_send()
+
+    spread = {}
+    others = (-1, 1, 2)
+
+    def quarter_of(dz_owner, half, start, size):
+        place = mc * HD + (mx if half == 0 else my) * STRIP + start
+        return down.at[(mz + dz_owner + SIDE) % SIDE, pl.ds(place, size), columns(half)]
+
+    def strip_send(half, index, dz_owner, start, size, step):
+        ref = quarter_of(dz_owner, half, start, size)
+        which = 2 + 2 * half
+        target = (me, ((mz + step + SIDE) % SIDE) * 2 + mc)
+        ring[which, index] = remote(ref, ref, w_ssem.at[which, index], w_rsem.at[which, index], target)
+
+    def shard_to_sibling(index, dz_owner):
+        ref = down.at[(mz + dz_owner + SIDE) % SIDE, pl.ds(mc * HD, HD), :]
+        ring[2, index] = remote(
+            ref, ref, w_ssem.at[2, index], w_rsem.at[2, index], (me, mz * 2 + 1 - mc)
+        )
+
+    def strip_spread(half, other):
+        ref = quarter_of(others[other], half, 0, STRIP)
+        for peer in range(3):
+            spread[half, other, peer] = remote(
+                ref,
+                ref,
+                s_ssem.at[half, other, peer],
+                s_rsem.at[half, other, peer],
+                (device(half, others[peer], 0), seq),
+            )
+
+    def output_1():
+        for half in range(2):
+            strip_send(half, 0, 0, 0, STRIP, 1)
+            strip_send(half, 1, 0, 0, STRIP, -1)
+        shard_to_sibling(4, 0)
+
+    def output_2():
+        for half in range(2):
+            ring[2 + 2 * half, 0].wait_recv()
+            strip_send(half, 2, -1, 0, STRIP // 2, 1)
+            strip_spread(half, 0)
+            ring[2 + 2 * half, 1].wait_recv()
+            strip_send(half, 3, 1, STRIP // 2, STRIP // 2, -1)
+            strip_spread(half, 1)
+
+    def output_3():
+        for half in range(2):
+            ring[2 + 2 * half, 2].wait_recv()
+            ring[2 + 2 * half, 3].wait_recv()
+            strip_spread(half, 2)
+
+    def output_4():
+        for other in range(3):
+            for half in range(2):
+                for peer in range(3):
+                    spread[half, other, peer].wait_recv()
+            shard_to_sibling(5 + other, others[other])
+
+    def output_5():
+        for index in range(4, 8):
+            ring[2, index].wait_recv()
+
+    def output_sent():
+        for copy in spread.values():
+            copy.wait_send()
+        for index in range(4):
+            ring[4, index].wait_send()
 
     def block(half, r1, r2):
         return device(half, r1, r2)
@@ -486,13 +554,19 @@
         for copy in stores[e]:
             copy.start()
 
-        @pl.loop(0, D // 256)
-        def _(j):
-            cols = pl.ds(pl.multiple_of(j * 256, 256), 256)
-            out = jnp.dot(hidden[...], down[e, :, cols], preferred_element_type=F32)
-            rows[e, :, 0:SRC, cols] = out.astype(BF16).reshape(N_DP, SRC, 256)
-            back = lax.dot_general(grads[...], gate_up[e, cols, :], NT, preferred_element_type=F32)
-            rows[e, :, SRC:BLK, cols] = back.astype(BF16).reshape(N_DP, SRC, 256)
+        for half in range(2):
+
+            @pl.loop(half * (HALF // 256), (half + 1) * (HALF // 256))
+            def _(j):
+                cols = pl.ds(pl.multiple_of(j * 256, 256), 256)
+                out = jnp.dot(hidden[...], down[e, :, cols], preferred_element_type=F32)
+                rows[e, :, 0:SRC, cols] = out.astype(BF16).reshape(N_DP, SRC, 256)
+                back = lax.dot_general(
+                    grads[...], gate_up[e, cols, :], NT, preferred_element_type=F32
+                )
+                rows[e, :, SRC:BLK, cols] = back.astype(BF16).reshape(N_DP, SRC, 256)
+
+            reduce_1(e, half)
 
     reduces = {}
 
@@ -504,16 +578,14 @@
     def part(e, half, r1, r2):
         return rows.at[e, block(half, r1, r2), :, columns(half)]
 
-    def reduce_1(e):
-        for half in range(2):
-            for r in range(4):
-                step = 1 if r < 2 else -1
-                reduce_send(e, half, r, part(e, half, r, 2), first_far.at[e, half, r], (0, step))
-        for half in range(2):
-            for r in (2, 3):
-                reduce_send(e, half, 4 + r, part(e, half, r, 1), first_near.at[e, half, 0, r], (0, 1))
-            for r in (0, 1):
-                reduce_send(e, half, 8 + r, part(e, half, r, -1), first_near.at[e, half, 1, r], (0, -1))
+    def reduce_1(e, half):
+        for r in range(4):
+            step = 1 if r < 2 else -1
+            reduce_send(e, half, r, part(e, half, r, 2), first_far.at[e, half, r], (0, step))
+        for r in (2, 3):
+            reduce_send(e, half, 4 + r, part(e, half, r, 1), first_near.at[e, half, 0, r], (0, 1))
+        for r in (0, 1):
+            reduce_send(e, half, 8 + r, part(e, half, r, -1), first_near.at[e, half, 1, r], (0, -1))
 
     def reduce_2(e):
         for r in range(4):
@@ -597,20 +669,22 @@
         [bias_ref[...], mem_session_ref[...].astype(F32), jnp.zeros((8 - KVH - 1, MEM), F32)],
         axis=0,
     )
-    own_loads[0].wait()
-    pl.semaphore_wait(barrier, 4 + N_SEQ - 1)
-
-    exchange_start(1)
+    for copy in own_loads:
+        copy.wait()
+    pl.semaphore_wait(barrier, 6 + N_SEQ - 1)
+
     meta_copies = []
     for offset in range(1, N_SEQ):
         peer = (seq + offset) % N_SEQ
         meta_copies.append(
             remote(meta.at[seq], meta.at[seq], m_ssem.at[offset], m_rsem.at[offset], (me, peer))
         )
+    output_1()
     ring_1(0)
-    for copy in own_loads[1:]:
-        copy.wait()
+    exchange_start(1)
+    output_2()
     ring_2(0)
+    output_3()
     ring_1(1)
     exchange_end(1)
     for e in range(OWN):
@@ -625,10 +699,10 @@
     for e in range(OWN):
         gather_2(1, e)
     ring_2(3)
-    ring_1(2)
     ring_3(1)
     for e in range(OWN):
         gather_3(1, e)
+    output_4()
     ring_3(3)
     ring_4(1)
     tokens = tokens_ref[...]
@@ -653,10 +727,7 @@
                 jnp.concatenate([first, second], axis=0), keys, values, bias, same
             )
             mixed.extend([both[0:TOK], both[TOK : 2 * TOK]])
-        if g == 0:
-            ring_2(2)
-    ring_3(2)
-    ring_4(2)
+    output_5()
     mixed = jnp.concatenate(mixed, axis=1)
     projected = jnp.dot(
         mixed, down[...].reshape((OWN + 1) * HID, D), preferred_element_type=F32
@@ -668,8 +739,9 @@
     either = (places[0] + places[1]).astype(BF16)
     exchange_build(0, jnp.dot(either, moe_in, preferred_element_type=F32).astype(BF16))
     exchange_start(0)
-    for which in range(4):
+    for which in (0, 1, 2, 3):
         ring_sent(which)
+    output_sent()
     load_start()
     for e in range(OWN):
         gather_4(1, e)
@@ -690,22 +762,19 @@
     gather_4(0, 2)
     gather_5(0, 0)
     compute(0)
-    reduce_1(0)
     gather_5(0, 1)
     compute(1)
     reduce_2(0)
-    reduce_1(1)
     gather_5(0, 2)
     compute(2)
-    reduce_1(2)
     reduce_2(1)
     reduce_3(0)
     reduce_2(2)
+    reduce_3(1)
     reduce_4(0)
-    reduce_3(1)
+    reduce_3(2)
     reduce_5(0)
     reduce_4(1)
-    reduce_3(2)
     reduce_4(2)
     reduce_5(1)
     reduce_5(2)
@@ -773,8 +842,10 @@
             dma((OWN, 3)),
             dma((N_SEQ,)),
             dma((N_SEQ,)),
-            dma((4, 8)),
-            dma((4, 8)),
+            dma((2, 3, 3)),
+            dma((2, 3, 3)),
+            dma((5, 8)),
+            dma((5, 8)),
             dma((2, N_SEQ)),
             dma((2, N_SEQ)),
             dma((OWN, N_SEQ)),

time: 268 us -> 258 us (0.963)
  Pallas kernels: 267 us -> 257 us
    pallas_call x1, Pallas kernels: 257 us -> 247 us  [decoder_block(): pl.pallas_call(block_kernel, out_shape=(jax.ShapeDtypeStruct((N_SEQ, OWN...]
where the time goes in v4:
time: 258 us
  Pallas kernels  257 us (100%)
    pallas_call x1, Pallas kernels, decoder_block(): pl.pallas_call(block_kernel, out_shape=(jax.ShapeDtypeStruct((N_SEQ, OWN...  247 us
    pallas_call x1, Pallas kernels, finish(): pl.pallas_call(finish_kernel, out_shape=(jax.ShapeDtypeStruct((TOK, D), B...  9.48 us

profile of v4, /device:TPU:1, one launch (start us, length us, event | category | flops | bytes accessed | tf_op | source)
XLA Modules:
  0.0 257.8 jit_solution(7768144619567995076)
XLA Ops:
  0.6 247.5 %decoder_block.1 = (bf16[8,48,2048]{2,1,0:T(8,128)(2,1)}, bf16[64,2048]{1,0:T(8,128)(2,1)}, bf16[3,2048,256]{2,1,0:T(8,128)(2,1)}, bf16[3,2048,256]{2,1,0:T(8,128)(2,1)}, bf16[3,256,2048]{2,1,0:T(8,128)(2,1)}) custom-call(bf16[64,2048]{1,0:T(8,128)(2,1)} %bitcast.16, f32[2,256]{1,0:T(2,128)} %bitcast.23, s32[1,256]{1,0:T(1,128)} %mem_session_ref.1, ...), custom_call_target="tpu_custom_call" | custom-call | tf_op jit(solution)/shard_map/decoder_block/pallas_call | solution.py:815
  248.1 9.5 %finish.1 = (bf16[64,2048]{1,0:T(8,128)(2,1)}, bf16[64,2048]{1,0:T(8,128)(2,1)}, bf16[3,2048,256]{2,1,0:T(8,128)(2,1)}, bf16[3,2048,256]{2,1,0:T(8,128)(2,1)}, bf16[3,256,2048]{2,1,0:T(8,128)(2,1)}) custom-call(s32[2,64]{1,0:T(2,128)} %bitcast.20, f32[2,64]{1,0:T(2,128)} %bitcast.22, bf16[8,48,2048]{2,1,0:T(8,128)(2,1)} %get-tuple-element.15.back_ref, ...), custom_call_target="tpu_custom_call" | custom-call | tf_op jit(solution)/shard_map/finish/pallas_call | solution.py:792

commit v5 on v4

--- a/solution.py
+++ b/solution.py
@@ -681,10 +681,10 @@
         )
     output_1()
     ring_1(0)
-    exchange_start(1)
     output_2()
     ring_2(0)
     output_3()
+    exchange_start(1)
     ring_1(1)
     exchange_end(1)
     for e in range(OWN):

time: 258 us -> 263 us (1.019)
  Pallas kernels: 257 us -> 262 us
    pallas_call x1, Pallas kernels: 247 us -> 252 us  [decoder_block(): pl.pallas_call(block_kernel, out_shape=(jax.ShapeDtypeStruct((N_SEQ, OWN...]
where the time goes in v5:
time: 263 us
  Pallas kernels  262 us (100%)
    pallas_call x1, Pallas kernels, decoder_block(): pl.pallas_call(block_kernel, out_shape=(jax.ShapeDtypeStruct((N_SEQ, OWN...  252 us
    pallas_call x1, Pallas kernels, finish(): pl.pallas_call(finish_kernel, out_shape=(jax.ShapeDtypeStruct((TOK, D), B...  9.48 us

profile of v5, /device:TPU:1, one launch (start us, length us, event | category | flops | bytes accessed | tf_op | source)
XLA Modules:
  0.0 262.5 jit_solution(11092205659044495673)
XLA Ops:
  0.6 252.2 %decoder_block.1 = (bf16[8,48,2048]{2,1,0:T(8,128)(2,1)}, bf16[64,2048]{1,0:T(8,128)(2,1)}, bf16[3,2048,256]{2,1,0:T(8,128)(2,1)}, bf16[3,2048,256]{2,1,0:T(8,128)(2,1)}, bf16[3,256,2048]{2,1,0:T(8,128)(2,1)}) custom-call(bf16[64,2048]{1,0:T(8,128)(2,1)} %bitcast.16, f32[2,256]{1,0:T(2,128)} %bitcast.23, s32[1,256]{1,0:T(1,128)} %mem_session_ref.1, ...), custom_call_target="tpu_custom_call" | custom-call | tf_op jit(solution)/shard_map/decoder_block/pallas_call | solution.py:815
  252.8 9.5 %finish.1 = (bf16[64,2048]{1,0:T(8,128)(2,1)}, bf16[64,2048]{1,0:T(8,128)(2,1)}, bf16[3,2048,256]{2,1,0:T(8,128)(2,1)}, bf16[3,2048,256]{2,1,0:T(8,128)(2,1)}, bf16[3,256,2048]{2,1,0:T(8,128)(2,1)}) custom-call(s32[2,64]{1,0:T(2,128)} %bitcast.20, f32[2,64]{1,0:T(2,128)} %bitcast.22, bf16[8,48,2048]{2,1,0:T(8,128)(2,1)} %get-tuple-element.15.back_ref, ...), custom_call_target="tpu_custom_call" | custom-call | tf_op jit(solution)/shard_map/finish/pallas_call | solution.py:792
